TPU v7x, 32 devices: a whole 2x2x4 slice. The times are simulated.
32 devices in a mesh: obj: 4 (over x, core), tile: 8 (over z, y).
Axes of the slice: x: 2, y: 2, z: 4, core: 2. Of those that a mesh axis runs over, the one named last changes fastest.
Arguments:
- checkpoints: bfloat16 [6, 12, 48, 8, 128], P(None, None, 'obj', 'tile'), may hold values from 0.19921875 to 2
- courant: float32 [2, 48, 8, 128], P(None, None, 'tile'), may hold values from -0.6 to 0.6
- insolation: float32 [8, 128], P('tile'), may hold values from 0.3 to 3
- region_mask: int32 [4, 8, 128], P('obj', 'tile'), may hold values 0 or 1
- measure_step: int32 [4], P('obj'), may hold values from 1 to 6
- snr_weight: float32 [12, 48], replicated, may hold values from 0.3 to 3
- diffusion_number: float32 [12, 47], replicated, may hold values from 0.1 to 2
- coupling: float32 [12, 12], replicated, may hold values from -1.75 to 1.75
- recombination: float32 [12], replicated, may hold values from 0.05 to 0.25
Outputs:
- state_adjoint: float32 [4, 12, 48, 8, 128], P('obj', None, None, 'tile')
- driver_grad: float32 [4, 6, 12, 48], P('obj')
All inputs are finite; a program needn't handle non-finite values. No bound on the sum of `region_mask` on one device may be relied on, other than what follows from the above.
Results may differ from a plain program's by a relative error of at most 0.0003.
Values may be sent and summed in bfloat16 or wider, within the bound.
No kernel may reach another device: no remote copies, remote signals or barrier semaphores. Data moves between devices by JAX's collectives and lax.ppermute only.
A program may use at most 64 MiB of HBM per device.

v0:
```python
import jax
import jax.numpy as jnp
from jax import lax
from jax.sharding import PartitionSpec as P

smoothing = 0.2


def padded_2(block, sides, width):
    for axis, dim in sides:
        count = lax.axis_size(axis)
        forward = [(i, i + 1) for i in range(count - 1)]
        forward.append((count - 1, 0))
        backward = [(target, source) for source, target in forward]
        low = lax.ppermute(
            lax.slice_in_dim(block, block.shape[dim] - width, None, axis=dim), axis, forward
        )
        high = lax.ppermute(lax.slice_in_dim(block, 0, width, axis=dim), axis, backward)
        block = jnp.concatenate([low, block, high], axis=dim)
    return block


def advect_back(adjoint, padded, flux, northward):
    lat_pad = jnp.pad(adjoint, ((0, 0), (0, 0), (0, 0), (1, 1)))
    north_flux = jnp.pad(northward[None] * adjoint, ((0, 0), (0, 0), (0, 0), (1, 1)))
    beside_all = padded[:, :, 2:] + padded[:, :, :-2] + lat_pad[..., 2:] + lat_pad[..., :-2]
    carried = flux[:, :, 2:] - flux[:, :, :-2] + north_flux[..., 2:] - north_flux[..., :-2]
    return (1.0 - 4.0 * smoothing) * adjoint + smoothing * beside_all + 0.5 * carried


def react_back(solved, state, coupling, recombination):
    mixing = jnp.einsum("fg,...flxy->...glxy", coupling, solved, precision=lax.Precision.HIGHEST)
    return (
        solved
        + mixing
        - 2.0 * recombination[:, None, None, None] * state.astype(jnp.float32) * solved
    )


def per_device(
    checkpoints,
    courant,
    insolation,
    region_mask,
    measure_step,
    snr_weight,
    diffusion_number,
    coupling,
    recombination,
):
    steps = checkpoints.shape[0]
    fields, levels = snr_weight.shape
    width, latitudes = insolation.shape
    columns = width * latitudes
    cells = columns * lax.axis_size("tile")
    impulse = region_mask[0].astype(jnp.float32)[None, None] * snr_weight[:, :, None, None]
    below = jnp.pad(diffusion_number, ((0, 0), (1, 0)))
    above = jnp.pad(diffusion_number, ((0, 0), (0, 1)))
    middle = 1.0 + below + above
    eastward = courant[0]
    northward = courant[1]
    adjoint = jnp.zeros((fields, levels, width, latitudes), jnp.float32)
    partials = [None] * steps
    for back in range(steps):
        moment = steps - 1 - back
        arrive = (measure_step[0] == moment + 1).astype(jnp.float32)
        adjoint = adjoint + arrive * impulse
        stacked = jnp.stack([adjoint, eastward[None] * adjoint])
        extended = padded_2(stacked, (("tile", 3),), 1)
        padded = extended[0]
        flux = extended[1]
        advected = advect_back(adjoint, padded, flux, northward)
        solved = lax.linalg.tridiagonal_solve(
            -below, middle, -above, advected.reshape(fields, levels, columns)
        )
        solved = solved.reshape(fields, levels, width, latitudes)
        partial_sum = jnp.einsum("flxy,xy->fl", solved, insolation, precision=lax.Precision.HIGHEST)
        partial_sum = lax.psum(partial_sum, "tile")
        partials[moment] = partial_sum
        state = checkpoints[moment]
        adjoint = react_back(
            solved, lax.all_gather(state, "obj", axis=1, tiled=True), coupling, recombination
        )
    gradients = jnp.stack(partials)
    return (adjoint[None], (gradients / cells)[None])


def solution(mesh):
    return jax.shard_map(
        per_device,
        mesh=mesh,
        in_specs=(
            P(None, None, "obj", "tile", None),
            P(None, None, "tile", None),
            P("tile", None),
            P("obj", "tile", None),
            P("obj"),
            P(),
            P(),
            P(),
            P(),
        ),
        out_specs=(P("obj", None, None, "tile", None), P("obj", None, None, None)),
        check_vma=False,
    )
```

profile of v0, /device:TPU:0, one launch (start us, length us, event | category | flops | bytes accessed | tf_op | source)
XLA Modules:
  0.0 245.0 jit_solution(2957823693080513006)
XLA Ops:
  1.4 0.7 convert_bitcast_fusion
  2.0 0.8 copy.28
  2.8 0.8 fusion.1314
  4.0 6.1 %collective-permute-start.1 = (f32[2,12,48,1,128]{4,2,3,1,0:T(8,128)S(1)}, f32[2,12,48,1,128]{4,2,3,1,0:T(8,128)S(1)}, u32[]{:S(2)}, u32[]{:S(2)}) collective-permute-start(f32[2,12,48,1,128]{4,2,3,1,0:T(8,128)S(1)} %copy.30), channel_id=1, source_target_pairs={{1,0},{2,1},{3,2},{4,3},{5,4},{6,5},{7,6},{0,7},{9,8},{10,9},{11,1... | collective-permute-start | bytes 1769480 | tf_op jit(solution)/shard_map/ppermute | solution.py:18
  10.4 0.4 fusion.1151
  10.8 0.4 fusion.1203
  11.3 5.6 %all-gather = bf16[1,12,48,1,128]{4,1,3,0,2:T(8,128)(2,1)S(1)} all-gather(bf16[1,12,12,1,128]{4,1,3,0,2:T(8,128)(2,1)S(1)} %copy.99), channel_id=2, replica_groups=mesh['obj'=4,'tile'=8] {'obj'}, dimensions={2}, use_global_device_ids=true | all-gather | bytes 184320 | tf_op jit(solution)/shard_map/all_gather | solution.py:82
  17.1 15.8 %collective-permute-done.1 = f32[2,12,48,1,128]{4,2,3,1,0:T(8,128)S(1)} collective-permute-done((f32[2,12,48,1,128]{4,2,3,1,0:T(8,128)S(1)}, f32[2,12,48,1,128]{4,2,3,1,0:T(8,128)S(1)}, u32[]{:S(2)}, u32[]{:S(2)}) %collective-permute-start.1) | collective-permute-done | bytes 589856 | tf_op jit(solution)/shard_map/ppermute | solution.py:18
  33.9 0.5 fusion.29
  34.4 0.5 fusion.1138
  34.9 0.4 constant_dynamic-update-slice_fusion.46
  36.9 0.4 constant_dynamic-update-slice_fusion.4
  37.6 0.6 fusion.13
  38.5 4.8 %collective-permute-start.3 = (f32[2,12,48,1,128]{4,2,3,1,0:T(8,128)S(1)}, f32[2,12,48,1,128]{4,2,3,1,0:T(8,128)S(1)}, u32[]{:S(2)}, u32[]{:S(2)}) collective-permute-start(f32[2,12,48,1,128]{4,2,3,1,0:T(8,128)S(1)} %copy.39), channel_id=1, source_target_pairs={{1,0},{2,1},{3,2},{4,3},{5,4},{6,5},{7,6},{0,7},{9,8},{10,9},{11,1... | collective-permute-start | bytes 1769480 | tf_op jit(solution)/shard_map/ppermute | solution.py:18
  43.3 5.6 %all-gather.1 = bf16[1,12,48,1,128]{4,1,3,0,2:T(8,128)(2,1)S(1)} all-gather(bf16[1,12,12,1,128]{4,1,3,0,2:T(8,128)(2,1)S(1)} %copy.100), channel_id=3, replica_groups=mesh['obj'=4,'tile'=8] {'obj'}, dimensions={2}, use_global_device_ids=true | all-gather | bytes 184320 | tf_op jit(solution)/shard_map/all_gather | solution.py:82
  48.9 18.2 %collective-permute-done.3 = f32[2,12,48,1,128]{4,2,3,1,0:T(8,128)S(1)} collective-permute-done((f32[2,12,48,1,128]{4,2,3,1,0:T(8,128)S(1)}, f32[2,12,48,1,128]{4,2,3,1,0:T(8,128)S(1)}, u32[]{:S(2)}, u32[]{:S(2)}) %collective-permute-start.3) | collective-permute-done | bytes 589856 | tf_op jit(solution)/shard_map/ppermute | solution.py:18
  67.8 0.3 slice_bitcast_fusion.9
  68.1 0.5 fusion.38
  68.6 0.5 fusion.959
  69.1 0.4 constant_dynamic-update-slice_fusion.93
  71.1 0.4 constant_dynamic-update-slice_fusion.51
  71.7 0.6 fusion.15
  72.6 3.1 %collective-permute-start.5 = (f32[2,12,48,1,128]{4,2,3,1,0:T(8,128)S(1)}, f32[2,12,48,1,128]{4,2,3,1,0:T(8,128)S(1)}, u32[]{:S(2)}, u32[]{:S(2)}) collective-permute-start(f32[2,12,48,1,128]{4,2,3,1,0:T(8,128)S(1)} %copy.46), channel_id=1, source_target_pairs={{1,0},{2,1},{3,2},{4,3},{5,4},{6,5},{7,6},{0,7},{9,8},{10,9},{11,1... | collective-permute-start | bytes 1769480 | tf_op jit(solution)/shard_map/ppermute | solution.py:18
  75.8 5.8 %all-gather.2 = bf16[1,12,48,1,128]{4,1,3,0,2:T(8,128)(2,1)S(1)} all-gather(bf16[1,12,12,1,128]{4,1,3,0,2:T(8,128)(2,1)S(1)} %copy.101), channel_id=4, replica_groups=mesh['obj'=4,'tile'=8] {'obj'}, dimensions={2}, use_global_device_ids=true | all-gather | bytes 184320 | tf_op jit(solution)/shard_map/all_gather | solution.py:82
  81.6 19.7 %collective-permute-done.5 = f32[2,12,48,1,128]{4,2,3,1,0:T(8,128)S(1)} collective-permute-done((f32[2,12,48,1,128]{4,2,3,1,0:T(8,128)S(1)}, f32[2,12,48,1,128]{4,2,3,1,0:T(8,128)S(1)}, u32[]{:S(2)}, u32[]{:S(2)}) %collective-permute-start.5) | collective-permute-done | bytes 589856 | tf_op jit(solution)/shard_map/ppermute | solution.py:18
  102.2 0.5 fusion.47
  102.8 0.5 fusion.786
  103.3 0.4 constant_dynamic-update-slice_fusion.140
  105.2 0.4 constant_dynamic-update-slice_fusion.98
  105.9 0.6 fusion.17
  106.8 1.4 collective-permute-start.7
  108.2 0.7 collective-permute-start.6
  109.0 5.6 %all-gather.5 = bf16[1,12,48,1,128]{4,1,3,0,2:T(8,128)(2,1)S(1)} all-gather(bf16[1,12,12,1,128]{4,1,3,0,2:T(8,128)(2,1)S(1)} %copy.104), channel_id=7, replica_groups=mesh['obj'=4,'tile'=8] {'obj'}, dimensions={2}, use_global_device_ids=true | all-gather | bytes 184320 | tf_op jit(solution)/shard_map/all_gather | solution.py:82
  114.6 5.6 %all-gather.3 = bf16[1,12,48,1,128]{4,1,3,0,2:T(8,128)(2,1)S(1)} all-gather(bf16[1,12,12,1,128]{4,1,3,0,2:T(8,128)(2,1)S(1)} %copy.102), channel_id=5, replica_groups=mesh['obj'=4,'tile'=8] {'obj'}, dimensions={2}, use_global_device_ids=true | all-gather | bytes 184320 | tf_op jit(solution)/shard_map/all_gather | solution.py:82
  120.2 5.6 %all-gather.4 = bf16[1,12,48,1,128]{4,1,3,0,2:T(8,128)(2,1)S(1)} all-gather(bf16[1,12,12,1,128]{4,1,3,0,2:T(8,128)(2,1)S(1)} %copy.103), channel_id=6, replica_groups=mesh['obj'=4,'tile'=8] {'obj'}, dimensions={2}, use_global_device_ids=true | all-gather | bytes 184320 | tf_op jit(solution)/shard_map/all_gather | solution.py:82
  125.8 0.9 fusion.84
  126.8 7.5 %collective-permute-done.7 = f32[2,12,48,1,128]{4,2,3,1,0:T(8,128)S(1)} collective-permute-done((f32[2,12,48,1,128]{4,2,3,1,0:T(8,128)S(1)}, f32[2,12,48,1,128]{4,2,3,1,0:T(8,128)S(1)}, u32[]{:S(2)}, u32[]{:S(2)}) %collective-permute-start.7) | collective-permute-done | bytes 589856 | tf_op jit(solution)/shard_map/ppermute | solution.py:18
  135.2 0.5 fusion.56
  135.7 0.5 fusion.613
  136.3 0.4 constant_dynamic-update-slice_fusion.187
  138.2 0.4 constant_dynamic-update-slice_fusion.145
  138.9 0.6 fusion.19
  139.8 2.6 %collective-permute-start.9 = (f32[2,12,48,1,128]{4,2,3,1,0:T(8,128)S(1)}, f32[2,12,48,1,128]{4,2,3,1,0:T(8,128)S(1)}, u32[]{:S(2)}, u32[]{:S(2)}) collective-permute-start(f32[2,12,48,1,128]{4,2,3,1,0:T(8,128)S(1)} %copy.60), channel_id=1, source_target_pairs={{1,0},{2,1},{3,2},{4,3},{5,4},{6,5},{7,6},{0,7},{9,8},{10,9},{11,1... | collective-permute-start | bytes 1769480 | tf_op jit(solution)/shard_map/ppermute | solution.py:18
  142.4 0.9 fusion.86
  143.4 0.9 fusion.88
  144.4 22.7 %collective-permute-done.9 = f32[2,12,48,1,128]{4,2,3,1,0:T(8,128)S(1)} collective-permute-done((f32[2,12,48,1,128]{4,2,3,1,0:T(8,128)S(1)}, f32[2,12,48,1,128]{4,2,3,1,0:T(8,128)S(1)}, u32[]{:S(2)}, u32[]{:S(2)}) %collective-permute-start.9) | collective-permute-done | bytes 589856 | tf_op jit(solution)/shard_map/ppermute | solution.py:18
  168.1 0.5 fusion.65
  168.6 0.5 fusion.440
  169.1 0.4 constant_dynamic-update-slice_fusion.234
  171.1 0.4 constant_dynamic-update-slice_fusion.192
  171.7 0.6 fusion.21
  172.6 3.9 %collective-permute-start.11 = (f32[2,12,48,1,128]{4,2,3,1,0:T(8,128)S(1)}, f32[2,12,48,1,128]{4,2,3,1,0:T(8,128)S(1)}, u32[]{:S(2)}, u32[]{:S(2)}) collective-permute-start(f32[2,12,48,1,128]{4,2,3,1,0:T(8,128)S(1)} %copy.67), channel_id=1, source_target_pairs={{1,0},{2,1},{3,2},{4,3},{5,4},{6,5},{7,6},{0,7},{9,8},{10,9},{11,1... | collective-permute-start | bytes 1769480 | tf_op jit(solution)/shard_map/ppermute | solution.py:18
  176.6 0.9 fusion.90
  177.6 0.9 fusion.92
  178.6 22.7 %collective-permute-done.11 = f32[2,12,48,1,128]{4,2,3,1,0:T(8,128)S(1)} collective-permute-done((f32[2,12,48,1,128]{4,2,3,1,0:T(8,128)S(1)}, f32[2,12,48,1,128]{4,2,3,1,0:T(8,128)S(1)}, u32[]{:S(2)}, u32[]{:S(2)}) %collective-permute-start.11) | collective-permute-done | bytes 589856 | tf_op jit(solution)/shard_map/ppermute | solution.py:18
  202.2 0.5 fusion.74
  202.8 0.5 fusion.267
  203.3 0.4 constant_dynamic-update-slice_fusion.281
  205.2 0.4 constant_dynamic-update-slice_fusion.239
  205.9 0.5 fusion.23
  206.5 1.0 copy.74
  207.5 0.9 fusion.94
  208.5 35.7 %all-reduce.14 = (f32[1,1,12,48]{3,0,2,1:T(1,128)S(1)}, f32[1,1,12,48]{3,0,2,1:T(1,128)S(1)}, f32[1,1,12,48]{3,0,2,1:T(1,128)S(1)}, f32[1,1,12,48]{3,0,2,1:T(1,1...) all-reduce(f32[1,1,12,48]{3,0,2,1:T(1,128)S(1)} %stack.87, ...), channel_id=1, replica_groups=mesh['obj'=4,'tile'=8] {'tile'}, use_global_device_ids=true, to_apply=%region_0.1 | all-reduce | flops 3456 | bytes 27648 | tf_op jit(solution)/shard_map/psum | solution.py:78
  244.3 0.6 broadcast_multiply_fusion.7
  (382 shorter events, 18.6 us)
Async XLA Ops:
  0.6 36.9 %copy-start = (f32[12,12]{1,0:T(8,128)S(1)}, f32[12,12]{1,0:T(8,128)}, u32[]{:S(2)}) copy-start(f32[12,12]{1,0:T(8,128)} %param.16) | copy-start | bytes 1732
  0.6 9.4 %copy-start.3 = (f32[12,47]{1,0:T(8,128)S(1)}, f32[12,47]{1,0:T(8,128)}, u32[]{:S(2)}) copy-start(f32[12,47]{1,0:T(8,128)} %param.15) | copy-start | bytes 6772
  0.7 10.6 %copy-start.1 = (bf16[6,12,12,1,128]{4,2,3,1,0:T(8,128)(2,1)S(1)}, bf16[6,12,12,1,128]{4,2,3,1,0:T(8,128)(2,1)}, u32[]{:S(2)}) copy-start(bf16[6,12,12,1,128]{4,2,3,1,0:T(8,128)(2,1)} %param.9) | copy-start | bytes 663556
  3.6 7.7 %copy-start.4 = (f32[12]{0:T(128)S(1)}, f32[12]{0:T(128)}, u32[]{:S(2)}) copy-start(f32[12]{0:T(128)} %param.17) | copy-start | bytes 148
  4.0 29.0 %collective-permute-start.1 = (f32[2,12,48,1,128]{4,2,3,1,0:T(8,128)S(1)}, f32[2,12,48,1,128]{4,2,3,1,0:T(8,128)S(1)}, u32[]{:S(2)}, u32[]{:S(2)}) collective-permute-start(f32[2,12,48,1,128]{4,2,3,1,0:T(8,128)S(1)} %copy.30), channel_id=1, source_target_pairs={{1,0},{2,1},{3,2},{4,3},{5,4},{6,5},{7,6},{0,7},{9,8},{10,9},{11,1... | collective-permute-start | bytes 1769480 | tf_op jit(solution)/shard_map/ppermute | solution.py:18
  10.0 23.1 %collective-permute-start = (f32[2,12,48,1,128]{4,2,3,1,0:T(8,128)S(1)}, f32[2,12,48,1,128]{4,2,3,1,0:T(8,128)S(1)}, u32[]{:S(2)}, u32[]{:S(2)}) collective-permute-start(f32[2,12,48,1,128]{4,2,3,1,0:T(8,128)S(1)} %copy.30), channel_id=1, source_target_pairs={{0,1},{1,2},{2,3},{3,4},{4,5},{5,6},{6,7},{7,0},{8,9},{9,10},{10,1... | collective-permute-start | bytes 1769480 | tf_op jit(solution)/shard_map/ppermute | solution.py:15
  38.5 28.6 %collective-permute-start.3 = (f32[2,12,48,1,128]{4,2,3,1,0:T(8,128)S(1)}, f32[2,12,48,1,128]{4,2,3,1,0:T(8,128)S(1)}, u32[]{:S(2)}, u32[]{:S(2)}) collective-permute-start(f32[2,12,48,1,128]{4,2,3,1,0:T(8,128)S(1)} %copy.39), channel_id=1, source_target_pairs={{1,0},{2,1},{3,2},{4,3},{5,4},{6,5},{7,6},{0,7},{9,8},{10,9},{11,1... | collective-permute-start | bytes 1769480 | tf_op jit(solution)/shard_map/ppermute | solution.py:18
  43.3 24.0 %collective-permute-start.2 = (f32[2,12,48,1,128]{4,2,3,1,0:T(8,128)S(1)}, f32[2,12,48,1,128]{4,2,3,1,0:T(8,128)S(1)}, u32[]{:S(2)}, u32[]{:S(2)}) collective-permute-start(f32[2,12,48,1,128]{4,2,3,1,0:T(8,128)S(1)} %copy.39), channel_id=1, source_target_pairs={{0,1},{1,2},{2,3},{3,4},{4,5},{5,6},{6,7},{7,0},{8,9},{9,10},{10,1... | collective-permute-start | bytes 1769480 | tf_op jit(solution)/shard_map/ppermute | solution.py:15
  72.6 28.6 %collective-permute-start.5 = (f32[2,12,48,1,128]{4,2,3,1,0:T(8,128)S(1)}, f32[2,12,48,1,128]{4,2,3,1,0:T(8,128)S(1)}, u32[]{:S(2)}, u32[]{:S(2)}) collective-permute-start(f32[2,12,48,1,128]{4,2,3,1,0:T(8,128)S(1)} %copy.46), channel_id=1, source_target_pairs={{1,0},{2,1},{3,2},{4,3},{5,4},{6,5},{7,6},{0,7},{9,8},{10,9},{11,1... | collective-permute-start | bytes 1769480 | tf_op jit(solution)/shard_map/ppermute | solution.py:18
  75.8 25.7 %collective-permute-start.4 = (f32[2,12,48,1,128]{4,2,3,1,0:T(8,128)S(1)}, f32[2,12,48,1,128]{4,2,3,1,0:T(8,128)S(1)}, u32[]{:S(2)}, u32[]{:S(2)}) collective-permute-start(f32[2,12,48,1,128]{4,2,3,1,0:T(8,128)S(1)} %copy.46), channel_id=1, source_target_pairs={{0,1},{1,2},{2,3},{3,4},{4,5},{5,6},{6,7},{7,0},{8,9},{9,10},{10,1... | collective-permute-start | bytes 1769480 | tf_op jit(solution)/shard_map/ppermute | solution.py:15
  106.6 19.2 %copy-start.2 = (f32[1,128]{1,0:T(1,128)S(1)}, f32[1,128]{1,0:T(1,128)}, u32[]{:S(2)}) copy-start(f32[1,128]{1,0:T(1,128)} %param.11) | copy-start | bytes 1540
  106.8 27.4 %collective-permute-start.7 = (f32[2,12,48,1,128]{4,2,3,1,0:T(8,128)S(1)}, f32[2,12,48,1,128]{4,2,3,1,0:T(8,128)S(1)}, u32[]{:S(2)}, u32[]{:S(2)}) collective-permute-start(f32[2,12,48,1,128]{4,2,3,1,0:T(8,128)S(1)} %copy.53), channel_id=1, source_target_pairs={{1,0},{2,1},{3,2},{4,3},{5,4},{6,5},{7,6},{0,7},{9,8},{10,9},{11,1... | collective-permute-start | bytes 1769480 | tf_op jit(solution)/shard_map/ppermute | solution.py:18
  108.2 26.2 %collective-permute-start.6 = (f32[2,12,48,1,128]{4,2,3,1,0:T(8,128)S(1)}, f32[2,12,48,1,128]{4,2,3,1,0:T(8,128)S(1)}, u32[]{:S(2)}, u32[]{:S(2)}) collective-permute-start(f32[2,12,48,1,128]{4,2,3,1,0:T(8,128)S(1)} %copy.53), channel_id=1, source_target_pairs={{0,1},{1,2},{2,3},{3,4},{4,5},{5,6},{6,7},{7,0},{8,9},{9,10},{10,1... | collective-permute-start | bytes 1769480 | tf_op jit(solution)/shard_map/ppermute | solution.py:15
  139.8 27.3 %collective-permute-start.9 = (f32[2,12,48,1,128]{4,2,3,1,0:T(8,128)S(1)}, f32[2,12,48,1,128]{4,2,3,1,0:T(8,128)S(1)}, u32[]{:S(2)}, u32[]{:S(2)}) collective-permute-start(f32[2,12,48,1,128]{4,2,3,1,0:T(8,128)S(1)} %copy.60), channel_id=1, source_target_pairs={{1,0},{2,1},{3,2},{4,3},{5,4},{6,5},{7,6},{0,7},{9,8},{10,9},{11,1... | collective-permute-start | bytes 1769480 | tf_op jit(solution)/shard_map/ppermute | solution.py:18
  142.4 24.9 %collective-permute-start.8 = (f32[2,12,48,1,128]{4,2,3,1,0:T(8,128)S(1)}, f32[2,12,48,1,128]{4,2,3,1,0:T(8,128)S(1)}, u32[]{:S(2)}, u32[]{:S(2)}) collective-permute-start(f32[2,12,48,1,128]{4,2,3,1,0:T(8,128)S(1)} %copy.60), channel_id=1, source_target_pairs={{0,1},{1,2},{2,3},{3,4},{4,5},{5,6},{6,7},{7,0},{8,9},{9,10},{10,1... | collective-permute-start | bytes 1769480 | tf_op jit(solution)/shard_map/ppermute | solution.py:15
  172.6 28.6 %collective-permute-start.11 = (f32[2,12,48,1,128]{4,2,3,1,0:T(8,128)S(1)}, f32[2,12,48,1,128]{4,2,3,1,0:T(8,128)S(1)}, u32[]{:S(2)}, u32[]{:S(2)}) collective-permute-start(f32[2,12,48,1,128]{4,2,3,1,0:T(8,128)S(1)} %copy.67), channel_id=1, source_target_pairs={{1,0},{2,1},{3,2},{4,3},{5,4},{6,5},{7,6},{0,7},{9,8},{10,9},{11,1... | collective-permute-start | bytes 1769480 | tf_op jit(solution)/shard_map/ppermute | solution.py:18
  176.6 24.9 %collective-permute-start.10 = (f32[2,12,48,1,128]{4,2,3,1,0:T(8,128)S(1)}, f32[2,12,48,1,128]{4,2,3,1,0:T(8,128)S(1)}, u32[]{:S(2)}, u32[]{:S(2)}) collective-permute-start(f32[2,12,48,1,128]{4,2,3,1,0:T(8,128)S(1)} %copy.67), channel_id=1, source_target_pairs={{0,1},{1,2},{2,3},{3,4},{4,5},{5,6},{6,7},{7,0},{8,9},{9,10},{10,1... | collective-permute-start | bytes 1769480 | tf_op jit(solution)/shard_map/ppermute | solution.py:15
where the time goes:
time: 245 us
  waiting for transfers between devices  107 us (44%)
  blocking collectives  69.5 us (28%)
  other arithmetic  26.3 us (11%)
  starting transfers between devices  22.6 us (9%)
  matrix products  9.09 us (4%)
  local copies, waits for them, and re-layouts  8.45 us (3%)
    ppermute x6, waiting for transfers between devices, padded_2(): lax.ppermute(lax.slice_in_dim(block, 0, width, axis=dim), axis, backward)  107 us
    psum x1, blocking collectives, per_device(): partial_sum = lax.psum(partial_sum, 'tile')  35.7 us
    all_gather x6, blocking collectives, per_device(): lax.all_gather(state, 'obj', axis=1, tiled=True)  33.8 us
    ppermute x6, starting transfers between devices, padded_2(): lax.ppermute(lax.slice_in_dim(block, 0, width, axis=dim), axis, backward)  21.9 us
    unnamed x144, other arithmetic  14.8 us
    dot_general x6, matrix products, per_device(): jnp.einsum('flxy,xy->fl', solved, insolation, precision=lax.Precision.HIG...  5.7 us
  transfers between devices with their start and end apart: 12, of which 6 were waited for; matrix products, arithmetic and copies ran while one was open for 3% of the time, Pallas kernels for 0%

commit v1 on v0

v1 whole, which is shorter than its diff:
```python
import functools

import jax
import jax.numpy as jnp
from jax import lax
from jax.experimental import pallas as pl
from jax.experimental.pallas import tpu as pltpu
from jax.sharding import PartitionSpec as P

smoothing = 0.2
lanes = 128
quads = 4
window = lanes // quads
exact = lax.Precision.HIGHEST


def up(value, unit):
    return -(-value // unit) * unit


def lane_iota(shape):
    return lax.broadcasted_iota(jnp.int32, shape, len(shape) - 1)


def pack_kernel(dims, checkpoints, courant, insolation, region_mask, out, staged):
    steps, groups, part, tiles, own, halo, rows = dims
    ours = lax.axis_index("obj") * part
    total = rows["all"]
    for quad in range(quads):
        for moment in range(steps):
            for group in range(groups):
                at = (moment * groups + group) * part
                staged[quad, at : at + part, :] = checkpoints[moment, group * quads + quad].astype(jnp.float32)
    for way in range(2):
        wind = courant[way, pl.ds(ours, part), :]
        coarse = wind.astype(jnp.bfloat16).astype(jnp.float32)
        staged[2 * way, rows["wind"] : rows["wind"] + part, :] = coarse
        staged[2 * way + 1, rows["wind"] : rows["wind"] + part, :] = wind - coarse
    light = insolation[...]
    coarse = light.astype(jnp.bfloat16).astype(jnp.float32)
    middle = (light - coarse).astype(jnp.bfloat16).astype(jnp.float32)
    cells = [region_mask[...].astype(jnp.float32), coarse, middle, light - coarse - middle]
    for quad in range(quads):
        staged[quad, rows["cells"] : rows["cells"] + 1, :] = cells[quad]
        staged[quad, rows["cells"] + 1 : total, :] = jnp.zeros((total - rows["cells"] - 1, lanes), jnp.float32)
    source = jnp.concatenate([staged[quad].astype(jnp.bfloat16) for quad in range(quads)], axis=1)
    for tile in range(tiles):
        shape = (quads * lanes, lanes)
        row = lax.broadcasted_iota(jnp.int32, shape, 0)
        lane = lane_iota(shape)
        wanted = (lane // window) * lanes + own * tile - halo + lane % window
        inside = own * tile - halo + lane % window
        pick = (row == wanted) & (inside >= 0) & (inside < lanes)
        pick = jnp.where(pick, 1.0, 0.0).astype(jnp.bfloat16)
        out[tile] = jnp.dot(source, pick, preferred_element_type=jnp.float32).astype(jnp.bfloat16)


def spread(values, group):
    fields = values.shape[0]
    shape = (fields, lanes)
    field = lax.broadcasted_iota(jnp.int32, shape, 0)
    chosen = jnp.where(field == group * quads + lane_iota(shape) // window, 1.0, 0.0)
    return lax.dot_general(
        values, chosen, (((0,), (0,)), ((), ())), precision=exact, preferred_element_type=jnp.float32
    )


def everywhere(quarter):
    quarter = jnp.where(lane_iota(quarter.shape) < window, quarter, 0.0)
    axis = len(quarter.shape) - 1
    quarter = quarter + pltpu.roll(quarter, window, axis)
    return quarter + pltpu.roll(quarter, 2 * window, axis)


def main_kernel(
    dims,
    measure_step,
    arrived,
    snr_weight,
    diffusion,
    coupling,
    recombination,
    out,
    wide,
    adjoint,
    solving,
    coefs,
    snr,
    multiplier,
    inverse,
    mixing,
    loss,
    sums,
):
    steps, groups, part, tiles, own, halo, rows, out_rows = dims
    total = rows["all"]
    fields, levels = snr_weight.shape
    parts = levels // part
    tile = lax.axis_index("tile")
    cell = (tiles, lanes)
    lane = lane_iota(cell)
    spot = lane % window
    latitude = own * tile - halo + spot
    inside = jnp.where((latitude >= 0) & (latitude < lanes), 1.0, 0.0)

    for piece in range(parts):
        for longitude in range(tiles):
            at = (piece * tiles + longitude) * total
            wide[at : at + total, :] = arrived[piece, longitude].astype(jnp.float32)

    def stored(piece, row):
        return wide[pl.ds(piece * (tiles * total) + row, tiles, stride=total), :]

    me = lax.axis_index("obj")
    misc = stored(me, rows["cells"])
    mask = everywhere(misc)
    light = misc + pltpu.roll(misc, lanes - window, 1) + pltpu.roll(misc, lanes - 2 * window, 1)
    light = everywhere(pltpu.roll(light, lanes - window, 1))
    light = jnp.where((spot >= halo) & (spot < halo + own), light, 0.0)

    for level in range(levels):
        both = stored(level // part, rows["wind"] + level % part)
        both = both + pltpu.roll(both, lanes - window, 1)
        east = everywhere(both)
        north = everywhere(pltpu.roll(both, lanes - 2 * window, 1))
        coefs[level, 0] = pltpu.roll(smoothing + 0.5 * east, tiles - 1, 0) * inside
        coefs[level, 1] = pltpu.roll(smoothing - 0.5 * east, 1, 0) * inside
        coefs[level, 2] = pltpu.roll(smoothing + 0.5 * north, lanes - 1, 1) * inside
        coefs[level, 3] = pltpu.roll(smoothing - 0.5 * north, 1, 1) * inside
    centre = (1.0 - 4.0 * smoothing) * inside

    for group in range(groups):
        snr[group] = spread(snr_weight[...], group)
        number = spread(diffusion[...], group)
        below = jnp.zeros((1, lanes), jnp.float32)
        last = jnp.ones((1, lanes), jnp.float32)
        earlier = jnp.zeros((1, lanes), jnp.float32)
        for level in range(levels):
            above = number[level : level + 1] if level < levels - 1 else jnp.zeros((1, lanes), jnp.float32)
            now = (1.0 + below + above) * last - below * below * earlier
            part_inverse = last / now
            inverse[group, level : level + 1, :] = part_inverse
            multiplier[group, level + 1 : level + 2, :] = above * part_inverse
            earlier = last
            last = now
            below = above
        multiplier[group, 0:1, :] = jnp.zeros((1, lanes), jnp.float32)

    shape = (fields, fields)
    identity = jnp.where(lax.broadcasted_iota(jnp.int32, shape, 0) == lax.broadcasted_iota(jnp.int32, shape, 1), 1.0, 0.0)
    across = jnp.transpose(coupling[...] + identity)
    for group in range(groups):
        columns = spread(across, group)
        quarter = lane_iota((1, lanes)) // window
        for source in range(groups):
            for turn in range(quads):
                line = jnp.zeros((1, lanes), jnp.float32)
                for quad in range(quads):
                    field = source * quads + (quad - turn) % quads
                    line = jnp.where(quarter == quad, columns[field : field + 1], line)
                at = (group * groups + source) * quads + turn
                mixing[at] = jnp.broadcast_to(line, (8, lanes))
        loss[group] = jnp.broadcast_to(-2.0 * spread(recombination[...], group), (8, lanes))

    adjoint[...] = jnp.zeros_like(adjoint)
    block = 4 if levels % 4 == 0 else 1

    def step(back, carry):
        moment = steps - 1 - back
        scored = jnp.where(measure_step[0] == moment + 1, 1.0, 0.0) * mask

        def forward(at, before):
            before = list(before)
            for inner in range(block):
                level = at * block + inner
                for group in range(groups):
                    value = adjoint[level * groups + group] + scored * snr[group, pl.ds(level, 1), :]
                    moved = centre * value
                    moved = moved + coefs[level, 0] * pltpu.roll(value, tiles - 1, 0)
                    moved = moved + coefs[level, 1] * pltpu.roll(value, 1, 0)
                    moved = moved + coefs[level, 2] * pltpu.roll(value, lanes - 1, 1)
                    moved = moved + coefs[level, 3] * pltpu.roll(value, 1, 1)
                    moved = moved + multiplier[group, pl.ds(level, 1), :] * before[group]
                    before[group] = moved
                    solving[level * groups + group] = moved * inverse[group, pl.ds(level, 1), :]
            return tuple(before)

        nothing = tuple(jnp.zeros(cell, jnp.float32) for _ in range(groups))
        lax.fori_loop(0, levels // block, forward, nothing)

        def backward(at, after):
            after = list(after)
            for inner in range(block):
                level = levels - 1 - (at * block + inner)
                turned = []
                for group in range(groups):
                    value = solving[level * groups + group]
                    value = value + multiplier[group, pl.ds(level + 1, 1), :] * after[group]
                    after[group] = value
                    lit = jnp.sum(value * light, axis=0, keepdims=True)
                    sums[pl.ds((moment * groups + group) * levels + level, 1), :] = lit
                    turned.append([value] + [pltpu.roll(value, window * turn, 1) for turn in range(1, quads)])
                for group in range(groups):
                    state = stored(level // part, (moment * groups + group) * part + level % part)
                    result = loss[group, 0:1] * state * after[group]
                    for source in range(groups):
                        for turn in range(quads):
                            place = (group * groups + source) * quads + turn
                            result = result + mixing[place, 0:1] * turned[source][turn]
                    adjoint[level * groups + group] = result
            return tuple(after)

        lax.fori_loop(0, levels // block, backward, nothing)
        return carry

    lax.fori_loop(0, steps, step, 0)

    stack = tiles // quads
    short = levels // stack
    home = lane // own
    for group in range(groups):
        for level in range(short):
            whole = jnp.zeros(cell, jnp.float32)
            for high in range(stack):
                value = adjoint[(high * short + level) * groups + group]
                for quad in range(quads):
                    target = (high * quads + quad) * own
                    turned = pltpu.roll(value, (target - quad * window - halo) % lanes, 1)
                    whole = jnp.where(home == high * quads + quad, turned, whole)
            out[pl.ds(group * short + level, tiles, stride=out_rows), :] = whole
    shape = (8, lanes)
    chosen = jnp.where(lax.broadcasted_iota(jnp.int32, shape, 0) == lane_iota(shape) // window, 1.0, 0.0)
    base = groups * short
    half = steps // 2
    for moment in range(half):
        for group in range(groups):
            pair = []
            for at in (moment, moment + half):
                place = (at * groups + group) * levels
                pair.append(
                    lax.dot_general(
                        chosen,
                        sums[place : place + levels, :],
                        (((1,), (1,)), ((), ())),
                        precision=exact,
                        preferred_element_type=jnp.float32,
                    )[:quads]
                )
            gap = jnp.zeros((quads, lanes // 2 - levels), jnp.float32)
            line = jnp.concatenate([pair[0], gap, pair[1], gap], axis=1)
            for longitude in range(tiles):
                at = longitude * out_rows + base + moment * fields + group * quads
                out[at : at + quads, :] = line
    for longitude in range(tiles):
        at = longitude * out_rows + base + half * fields
        out[at : (longitude + 1) * out_rows, :] = jnp.zeros((out_rows - base - half * fields, lanes), jnp.float32)


def unpack_kernel(dims, arrived, state_adjoint, driver_grad):
    steps, groups, levels, fields, tiles, own, cells = dims
    stack = tiles // quads
    short = levels // stack
    base = groups * short
    half = steps // 2
    values = [arrived[tile, 0:base, :] for tile in range(tiles)]
    home = lane_iota((base, lanes)) // own
    apart = 1
    while apart < tiles:
        for low in range(tiles):
            if low & apart:
                continue
            first, second = values[low], values[low + apart]
            here = (home & apart) == 0
            values[low] = jnp.where(here, first, pltpu.roll(second, apart * own, 1))
            values[low + apart] = jnp.where(here, pltpu.roll(first, lanes - apart * own, 1), second)
        apart *= 2
    for high in range(stack):
        for quad in range(quads):
            for group in range(groups):
                at = (group * quads + quad) * levels + high * short
                state_adjoint[at : at + short, :] = values[high * quads + quad][group * short : (group + 1) * short]
    total = arrived[0, base : base + half * fields, :]
    for tile in range(1, tiles):
        total = total + arrived[tile, base : base + half * fields, :]
    total = total / cells
    late = pltpu.roll(total, lanes // 2, 1)
    for moment in range(half):
        driver_grad[moment] = total[moment * fields : (moment + 1) * fields, :levels]
        driver_grad[moment + half] = late[moment * fields : (moment + 1) * fields, :levels]


def per_device(
    checkpoints,
    courant,
    insolation,
    region_mask,
    measure_step,
    snr_weight,
    diffusion_number,
    coupling,
    recombination,
):
    steps, fields, part = checkpoints.shape[:3]
    levels = snr_weight.shape[1]
    tiles = lax.axis_size("tile")
    parts = levels // part
    groups = fields // quads
    own = lanes // tiles
    halo = (window - own) // 2
    rows = {"wind": steps * groups * part}
    rows["cells"] = rows["wind"] + part
    rows["all"] = up(rows["cells"] + 1, 16)
    total = rows["all"]
    short = levels // (tiles // quads)
    out_rows = up(groups * short + steps // 2 * fields, 8)
    limit = pltpu.CompilerParams(vmem_limit_bytes=48 * 2**20)
    in_vmem = pl.BlockSpec(memory_space=pltpu.VMEM)
    in_smem = pl.BlockSpec(memory_space=pltpu.SMEM)
    f32 = jnp.float32

    packed = pl.pallas_call(
        functools.partial(pack_kernel, (steps, groups, part, tiles, own, halo, rows)),
        out_shape=jax.ShapeDtypeStruct((tiles, total, lanes), jnp.bfloat16),
        in_specs=[in_vmem] * 4,
        out_specs=in_vmem,
        scratch_shapes=[pltpu.VMEM((quads, total, lanes), f32)],
        compiler_params=limit,
    )(
        checkpoints.reshape(steps, fields, part, lanes),
        courant.reshape(2, levels, lanes),
        insolation,
        region_mask.reshape(1, lanes),
    )
    strips = lax.all_to_all(packed, "tile", 0, 0, tiled=True)
    arrived = lax.all_gather(strips, "obj", axis=0, tiled=False)

    cell = (tiles, lanes)
    result = pl.pallas_call(
        functools.partial(main_kernel, (steps, groups, part, tiles, own, halo, rows, out_rows)),
        out_shape=jax.ShapeDtypeStruct((tiles * out_rows, lanes), f32),
        in_specs=[in_smem] + [in_vmem] * 5,
        out_specs=in_vmem,
        scratch_shapes=[
            pltpu.VMEM((parts * tiles * total, lanes), f32),
            pltpu.VMEM((levels * groups,) + cell, f32),
            pltpu.VMEM((levels * groups,) + cell, f32),
            pltpu.VMEM((levels, 4) + cell, f32),
            pltpu.VMEM((groups, levels, lanes), f32),
            pltpu.VMEM((groups, levels + 8, lanes), f32),
            pltpu.VMEM((groups, levels, lanes), f32),
            pltpu.VMEM((groups * groups * quads, 8, lanes), f32),
            pltpu.VMEM((groups, 8, lanes), f32),
            pltpu.VMEM((steps * groups * levels, lanes), f32),
        ],
        compiler_params=limit,
    )(
        measure_step,
        arrived,
        snr_weight,
        diffusion_number,
        coupling,
        recombination.reshape(fields, 1),
    )
    home = lax.all_to_all(result.reshape(tiles, out_rows, lanes), "tile", 0, 0, tiled=True)

    state_adjoint, driver_grad = pl.pallas_call(
        functools.partial(unpack_kernel, (steps, groups, levels, fields, tiles, own, tiles * lanes)),
        out_shape=(
            jax.ShapeDtypeStruct((fields * levels, lanes), f32),
            jax.ShapeDtypeStruct((steps, fields, levels), f32),
        ),
        in_specs=[in_vmem],
        out_specs=(in_vmem, in_vmem),
        compiler_params=limit,
    )(home)
    return (state_adjoint.reshape(1, fields, levels, 1, lanes), driver_grad[None])


def solution(mesh):
    return jax.shard_map(
        per_device,
        mesh=mesh,
        in_specs=(
            P(None, None, "obj", "tile", None),
            P(None, None, "tile", None),
            P("tile", None),
            P("obj", "tile", None),
            P("obj"),
            P(),
            P(),
            P(),
            P(),
        ),
        out_specs=(P("obj", None, None, "tile", None), P("obj", None, None, None)),
        check_vma=False,
    )
```

time: 245 us -> 100 us (0.41)
  waiting for transfers between devices: 107 us -> 20.3 us
  blocking collectives: 69.5 us -> 39.9 us
  other arithmetic: 26.3 us -> 0 us
  starting transfers between devices: 22.6 us -> 0.04 us
  Pallas kernels: 0 us -> 19.7 us
  between operations: 2.37 us -> 14.7 us
  matrix products: 9.09 us -> 0 us
  local copies, waits for them, and re-layouts: 8.45 us -> 5.37 us
    ppermute x12 -> x0, waiting for transfers between devices: 107 us -> none  [the longest x6 107 us: padded_2(): lax.ppermute(lax.slice_in_dim(block, 0, width, axis=dim), axis, backward)]
    all_to_all x0 -> x2, blocking collectives: none -> 39.9 us  [the longest x1 21 us: per_device(): strips = lax.all_to_all(packed, 'tile', 0, 0, tiled=True)]
    psum x1 -> x0, blocking collectives: 35.7 us -> none  [per_device(): partial_sum = lax.psum(partial_sum, 'tile')]
    all_gather x6 -> x0, blocking collectives: 33.8 us -> none  [per_device(): lax.all_gather(state, 'obj', axis=1, tiled=True)]
    ppermute x12 -> x0, starting transfers between devices: 22.6 us -> none  [the longest x6 21.9 us: padded_2(): lax.ppermute(lax.slice_in_dim(block, 0, width, axis=dim), axis, backward)]
    all_gather x0 -> x1, waiting for transfers between devices: none -> 20.3 us  [per_device(): arrived = lax.all_gather(strips, 'obj', axis=0, tiled=False)]
    pallas_call x0 -> x3, Pallas kernels: none -> 19.7 us  [the longest x1 18 us: per_device(): pl.pallas_call(functools.partial(main_kernel, (steps, groups, part, tiles...]
    unnamed x144 -> x0, other arithmetic: 14.8 us -> none
  transfers between devices with their start and end apart: 12 -> 1, of which waited for: 6 -> 1; matrix products, arithmetic and copies ran while one was open for 3% -> 0% of each run, Pallas kernels for 0% -> 0%
where the time goes in v1:
time: 100 us
  blocking collectives  39.9 us (40%)
  waiting for transfers between devices  20.3 us (20%)
  Pallas kernels  19.7 us (20%)
  between operations  14.7 us (15%)
  local copies, waits for them, and re-layouts  5.37 us (5%)
    all_to_all x1, blocking collectives, per_device(): strips = lax.all_to_all(packed, 'tile', 0, 0, tiled=True)  21 us
    all_gather x1, waiting for transfers between devices, per_device(): arrived = lax.all_gather(strips, 'obj', axis=0, tiled=False)  20.3 us
    all_to_all x1, blocking collectives, per_device(): lax.all_to_all(result.reshape(tiles, out_rows, lanes), 'tile', 0, 0, tile...  18.9 us
    pallas_call x1, Pallas kernels, per_device(): pl.pallas_call(functools.partial(main_kernel, (steps, groups, part, tiles...  18 us
    unnamed x19, local copies, waits for them, and re-layouts  5.27 us
  transfers between devices with their start and end apart: 1, of which 1 were waited for; matrix products, arithmetic and copies ran while one was open for 0% of the time, Pallas kernels for 0%

profile of v1, /device:TPU:0, one launch (start us, length us, event | category | flops | bytes accessed | tf_op | source)
XLA Modules:
  0.0 100.0 jit_solution(5450298740614764362)
XLA Ops:
  7.2 0.0 copy-start.8
  7.2 0.0 all-gather.3.cloned.1.call-start
  7.2 0.0 copy-start.1
  7.2 1.0 copy-done.1
  8.2 0.0 copy-start.2
  8.2 0.8 copy-done.2
  9.0 0.0 copy-start.6
  9.0 0.7 copy-done.6
  9.6 0.0 copy-start.7
  9.6 0.7 copy-done.7
  10.3 0.0 copy-start.3
  10.3 0.0 copy-start.4
  10.3 0.0 copy-start.5
  10.3 0.7 shard_map.104
  11.0 21.0 %all_to_all.10 = bf16[8,240,128]{2,1,0:T(8,128)(2,1)} all-to-all(bf16[8,240,128]{2,1,0:T(8,128)(2,1)S(1)} %shard_map.104), channel_id=1, replica_groups=mesh['obj'=4,'tile'=8] {'tile'}, dimensions={0} | all-to-all | bytes 983040 | tf_op jit(solution)/shard_map/all_to_all | solution.py:334
  32.0 0.0 all-gather.3.cloned.1.call-update
  32.0 0.0 copy-done.8
  32.0 0.1 copy.14.recombination
  32.8 20.3 %all-gather.3.cloned.1.call-done = bf16[32,240,128]{2,1,0:T(8,128)(2,1)} async-done(((bf16[8,240,128]{2,1,0:T(8,128)(2,1)}), bf16[32,240,128]{2,1,0:T(8,128)(2,1)}) %all-gather.3.cloned.1.call-update) | async-done | bytes 1966096 | tf_op jit(solution)/shard_map/all_gather | solution.py:335
  53.0 0.0 copy-done.3
  53.0 0.0 copy-done.4
  53.0 0.0 copy-done.5
  53.0 0.0 copy-start
  53.1 1.5 %copy-done = bf16[32,240,128]{2,1,0:T(8,128)(2,1)S(1)} copy-done((bf16[32,240,128]{2,1,0:T(8,128)(2,1)S(1)}, bf16[32,240,128]{2,1,0:T(8,128)(2,1)}, u32[]{:S(2)}) %copy-start) | copy-done | bytes 1966104
  54.6 18.0 %shard_map.105 = f32[896,128]{1,0:T(8,128)S(1)} custom-call(s32[1]{0:T(128)S(6)} %copy.17.measure_step, bf16[4,8,240,128]{3,2,1,0:T(8,128)(2,1)S(1)} %bitcast.10, f32[12,48]{1,0:T(8,128)S(1)} %copy-done.3, f32[12,47]{1,0:T(8,128)S(1)} %copy-done.4, f32[12,12]{1,0:T(8,128)S(1)} %copy-done.5, f32[12,1]{1,0:T(8,128)S(1)} %copy.14.recombination), custom_call_target="tpu_custom_call" | custom-call | tf_op jit(solution)/shard_map/pallas_call | solution.py:338
  72.6 18.9 %all_to_all.11.arrived = f32[8,112,128]{2,1,0:T(8,128)S(1)} all-to-all(f32[8,112,128]{2,1,0:T(8,128)S(1)} %bitcast.11), channel_id=1, replica_groups=mesh['obj'=4,'tile'=8] {'tile'}, dimensions={0} | all-to-all | bytes 917504 | tf_op jit(solution)/shard_map/all_to_all | solution.py:364
  91.5 1.0 %shard_map.106 = (f32[576,128]{1,0:T(8,128)}, f32[6,12,48]{2,1,0:T(8,128)S(1)}) custom-call(f32[8,112,128]{2,1,0:T(8,128)S(1)} %all_to_all.11.arrived), custom_call_target="tpu_custom_call" | custom-call | tf_op jit(solution)/shard_map/pallas_call | solution.py:366
  92.5 0.7 copy.16
Async XLA Ops:
  7.2 24.9 %copy-start.8 = (f32[12]{0:T(128)S(1)}, f32[12]{0:T(128)}, u32[]{:S(2)}) copy-start(f32[12]{0:T(128)} %param.17) | copy-start | bytes 148
  7.2 45.9 %all-gather.3.cloned.1.call-start = ((), (), s32[]{:S(2)}) async-start(), calls=%async_computation.2 | async-start | bytes 2457600 | tf_op jit(solution)/shard_map/all_gather | solution.py:335
  7.2 1.0 copy-start.1
  8.2 0.8 copy-start.2
  9.0 0.7 copy-start.6
  9.6 0.7 copy-start.7
  10.3 42.7 %copy-start.3 = (f32[12,48]{1,0:T(8,128)S(1)}, f32[12,48]{1,0:T(8,128)}, u32[]{:S(2)}) copy-start(f32[12,48]{1,0:T(8,128)} %snr_weight.1) | copy-start | bytes 6916
  10.3 42.7 %copy-start.4 = (f32[12,47]{1,0:T(8,128)S(1)}, f32[12,47]{1,0:T(8,128)}, u32[]{:S(2)}) copy-start(f32[12,47]{1,0:T(8,128)} %diffusion.1) | copy-start | bytes 6772
  10.3 42.7 %copy-start.5 = (f32[12,12]{1,0:T(8,128)S(1)}, f32[12,12]{1,0:T(8,128)}, u32[]{:S(2)}) copy-start(f32[12,12]{1,0:T(8,128)} %coupling.1) | copy-start | bytes 1732
  53.0 1.5 %copy-start = (bf16[32,240,128]{2,1,0:T(8,128)(2,1)S(1)}, bf16[32,240,128]{2,1,0:T(8,128)(2,1)}, u32[]{:S(2)}) copy-start(bf16[32,240,128]{2,1,0:T(8,128)(2,1)} %all-gather.3.cloned.1.call-done) | copy-start | bytes 5898244
Sparse Core Ops, SparseCore 0:
  32.1 20.8 all-gather.2

commit v2 on v1

v2 whole, which is shorter than its diff:
```python
import functools

import jax
import jax.numpy as jnp
from jax import lax
from jax.experimental import pallas as pl
from jax.experimental.pallas import tpu as pltpu
from jax.sharding import PartitionSpec as P

smoothing = 0.2
lanes = 128
quads = 4
window = lanes // quads
exact = lax.Precision.HIGHEST


def up(value, unit):
    return -(-value // unit) * unit


def lane_iota(shape):
    return lax.broadcasted_iota(jnp.int32, shape, len(shape) - 1)


def pack_kernel(dims, rows, spots, checkpoints, courant, insolation, region_mask, out, staged):
    steps, groups, part, tiles, own, halo = dims
    count = steps // 2
    ours = lax.axis_index("obj") * part
    total = sum(rows)
    for quad in range(quads):
        for back in range(steps):
            base = back * groups * part if back < count else rows[0] + (back - count) * groups * part
            for group in range(groups):
                at = base + group * part
                state = checkpoints[steps - 1 - back, group * quads + quad]
                staged[quad, at : at + part, :] = state.astype(jnp.float32)
    for way in range(2):
        wind = courant[way, pl.ds(ours, part), :]
        coarse = wind.astype(jnp.bfloat16).astype(jnp.float32)
        staged[2 * way, spots["wind"] : spots["wind"] + part, :] = coarse
        staged[2 * way + 1, spots["wind"] : spots["wind"] + part, :] = wind - coarse
    light = insolation[...]
    coarse = light.astype(jnp.bfloat16).astype(jnp.float32)
    middle = (light - coarse).astype(jnp.bfloat16).astype(jnp.float32)
    cells = [region_mask[...].astype(jnp.float32), coarse, middle, light - coarse - middle]
    ends = rows[0] + (steps - count) * groups * part
    for quad in range(quads):
        staged[quad, spots["cells"] : spots["cells"] + 1, :] = cells[quad]
        if spots["cells"] + 1 < rows[0]:
            rest = rows[0] - spots["cells"] - 1
            staged[quad, spots["cells"] + 1 : rows[0], :] = jnp.zeros((rest, lanes), jnp.float32)
        if ends < total:
            staged[quad, ends:total, :] = jnp.zeros((total - ends, lanes), jnp.float32)
    source = jnp.concatenate([staged[quad].astype(jnp.bfloat16) for quad in range(quads)], axis=1)
    for tile in range(tiles):
        shape = (quads * lanes, lanes)
        row = lax.broadcasted_iota(jnp.int32, shape, 0)
        lane = lane_iota(shape)
        wanted = (lane // window) * lanes + own * tile - halo + lane % window
        inside = own * tile - halo + lane % window
        pick = (row == wanted) & (inside >= 0) & (inside < lanes)
        pick = jnp.where(pick, 1.0, 0.0).astype(jnp.bfloat16)
        out[tile] = jnp.dot(source, pick, preferred_element_type=jnp.float32).astype(jnp.bfloat16)


def spread(values, group):
    fields = values.shape[0]
    shape = (fields, lanes)
    field = lax.broadcasted_iota(jnp.int32, shape, 0)
    chosen = jnp.where(field == group * quads + lane_iota(shape) // window, 1.0, 0.0)
    return lax.dot_general(
        values, chosen, (((0,), (0,)), ((), ())), precision=exact, preferred_element_type=jnp.float32
    )


def everywhere(quarter):
    quarter = jnp.where(lane_iota(quarter.shape) < window, quarter, 0.0)
    axis = len(quarter.shape) - 1
    quarter = quarter + pltpu.roll(quarter, window, axis)
    return quarter + pltpu.roll(quarter, 2 * window, axis)


def prepare_kernel(
    tiles, snr_weight, diffusion, coupling, recombination, snr, multiplier, inverse, mixing, loss, number, ratio
):
    fields, levels = snr_weight.shape
    groups = fields // quads
    cell = (tiles, lanes)
    for group in range(groups):
        spreaded = spread(snr_weight[...], group)
        for level in range(levels):
            snr[level * groups + group] = jnp.broadcast_to(spreaded[level : level + 1], cell)
        above = spread(diffusion[...], group)
        number[pl.ds(group, levels - 1, stride=8), :] = above
        number[pl.ds((levels - 1) * 8 + group, 1), :] = jnp.zeros((1, lanes), jnp.float32)

    valid = lax.broadcasted_iota(jnp.int32, (8, lanes), 0) < groups
    below = jnp.zeros((8, lanes), jnp.float32)
    last = jnp.ones((8, lanes), jnp.float32)
    earlier = jnp.zeros((8, lanes), jnp.float32)
    for level in range(levels):
        above = jnp.where(valid, number[level * 8 : level * 8 + 8, :], 0.0)
        now = (1.0 + below + above) * last - (below * below) * earlier
        turned = last / now
        ratio[level * 8 : level * 8 + 8, :] = turned
        number[level * 8 : level * 8 + 8, :] = above * turned
        earlier = last
        last = now
        below = above
    for group in range(groups):
        multiplier[group] = jnp.zeros(cell, jnp.float32)
        for level in range(levels):
            inverse[level * groups + group] = jnp.broadcast_to(ratio[level * 8 + group : level * 8 + group + 1, :], cell)
            multiplier[(level + 1) * groups + group] = jnp.broadcast_to(
                number[level * 8 + group : level * 8 + group + 1, :], cell
            )

    shape = (fields, fields)
    identity = jnp.where(lax.broadcasted_iota(jnp.int32, shape, 0) == lax.broadcasted_iota(jnp.int32, shape, 1), 1.0, 0.0)
    across = jnp.transpose(coupling[...] + identity)
    quarter = lane_iota((1, lanes)) // window
    for group in range(groups):
        columns = spread(across, group)
        for source in range(groups):
            for turn in range(quads):
                line = jnp.zeros((1, lanes), jnp.float32)
                for quad in range(quads):
                    field = source * quads + (quad - turn) % quads
                    line = jnp.where(quarter == quad, columns[field : field + 1], line)
                at = (group * groups + source) * quads + turn
                mixing[at] = jnp.broadcast_to(line, cell)
        loss[group] = jnp.broadcast_to(-2.0 * spread(recombination[...], group), cell)


def widen(dims, rows, pieces, wide):
    tiles = dims[3]
    me = lax.axis_index("obj")
    for apart, piece in enumerate(pieces):
        start = (me ^ apart) * (tiles * rows)
        for longitude in range(tiles):
            at = pl.multiple_of(start + longitude * rows, 8)
            wide[pl.ds(at, rows), :] = piece[longitude].astype(jnp.float32)


def steps_back(dims, rows, measure_step, first, count, mask, light, tables, wide, adjoint, coefs, sums, solving, lit):
    steps, groups, part, tiles, own, halo = dims
    snr, multiplier, inverse, mixing, loss = tables
    levels = adjoint.shape[0] // groups
    cell = (tiles, lanes)
    latitude = own * lax.axis_index("tile") - halo + lane_iota(cell) % window
    inside = jnp.where((latitude >= 0) & (latitude < lanes), 1.0, 0.0)
    centre = (1.0 - 4.0 * smoothing) * inside
    block = 12 if levels % 12 == 0 else 2
    nothing = tuple(jnp.zeros(cell, jnp.float32) for _ in range(groups))

    def step(back, carry):
        moment = first - back
        upcoming = jnp.where((measure_step[0] == moment) & (moment > 0), 1.0, 0.0)
        scored = upcoming * mask

        def forward(at, before):
            before = list(before)
            for inner in range(block):
                level = at * block + inner
                for group in range(groups):
                    row = level * groups + group
                    value = adjoint[row, 0:tiles]
                    moved = centre * value
                    moved = moved + coefs[level, 0] * adjoint[row, 1 : tiles + 1]
                    moved = moved + coefs[level, 1] * adjoint[row, tiles - 1 : 2 * tiles - 1]
                    moved = moved + coefs[level, 2] * pltpu.roll(value, lanes - 1, 1)
                    moved = moved + coefs[level, 3] * pltpu.roll(value, 1, 1)
                    moved = moved + multiplier[row] * before[group]
                    before[group] = moved
                    solving[row] = moved * inverse[row]
            return tuple(before)

        lax.fori_loop(0, levels // block, forward, nothing)

        def backward(at, after):
            after = list(after)
            for inner in range(0, block, 2):
                pair = [levels - 1 - (at * block + inner), levels - 2 - (at * block + inner)]
                turned = []
                states = []
                for level in pair:
                    shifted = []
                    state = []
                    for group in range(groups):
                        row = level * groups + group
                        value = solving[row] + multiplier[row + groups] * after[group]
                        after[group] = value
                        lit[pl.ds(pl.multiple_of(row * tiles, 8), tiles), :] = value * light
                        shifted.append([value] + [pltpu.roll(value, window * turn, 1) for turn in range(1, quads)])
                        start = (level // part) * (tiles * rows) + (back * groups + group) * part + level % part
                        state.append(wide[pl.ds(start, tiles, stride=rows), :])
                    turned.append(shifted)
                    states.append(state)
                for group in range(groups):
                    result = [
                        loss[group] * states[at_pair][group] * turned[at_pair][group][0]
                        + scored * snr[pair[at_pair] * groups + group]
                        for at_pair in range(2)
                    ]
                    for source in range(groups):
                        for turn in range(quads):
                            factor = mixing[(group * groups + source) * quads + turn]
                            for at_pair in range(2):
                                result[at_pair] = result[at_pair] + factor * turned[at_pair][source][turn]
                    for at_pair in range(2):
                        row = pair[at_pair] * groups + group
                        adjoint[row, 0:tiles] = result[at_pair]
                        adjoint[row, tiles : 2 * tiles] = result[at_pair]
            return tuple(after)

        lax.fori_loop(0, levels // block, backward, nothing)
        for eight in range(levels * groups // 8):
            total = lit[pl.ds(eight * 8 * tiles, 8, stride=tiles), :]
            for longitude in range(1, tiles):
                total = total + lit[pl.ds(eight * 8 * tiles + longitude, 8, stride=tiles), :]
            sums[pl.ds(pl.multiple_of(back * (levels * groups) + eight * 8, 8), 8), :] = total
        return carry

    lax.fori_loop(0, count, step, 0)


def early_kernel(dims, rows, spots, count, parts, measure_step, *refs):
    pieces, refs = refs[:parts], refs[parts:]
    tables, refs = refs[:5], refs[5:]
    adjoint, coefs, sums, cells, wide, solving, lit = refs
    steps, groups, part, tiles, own, halo = dims
    levels = adjoint.shape[0] // groups
    widen(dims, rows, pieces, wide)
    cell = (tiles, lanes)
    spot = lane_iota(cell) % window
    latitude = own * lax.axis_index("tile") - halo + spot
    inside = jnp.where((latitude >= 0) & (latitude < lanes), 1.0, 0.0)

    def stored(piece, row):
        return wide[pl.ds(piece * (tiles * rows) + row, tiles, stride=rows), :]

    misc = stored(lax.axis_index("obj"), spots["cells"])
    mask = everywhere(misc)
    light = misc + pltpu.roll(misc, lanes - window, 1) + pltpu.roll(misc, lanes - 2 * window, 1)
    light = everywhere(pltpu.roll(light, lanes - window, 1))
    light = jnp.where((spot >= halo) & (spot < halo + own), light, 0.0)
    cells[0] = mask
    cells[1] = light

    for level in range(levels):
        both = stored(level // part, spots["wind"] + level % part)
        both = both + pltpu.roll(both, lanes - window, 1)
        east = everywhere(both)
        north = everywhere(pltpu.roll(both, lanes - 2 * window, 1))
        coefs[level, 0] = pltpu.roll(smoothing + 0.5 * east, tiles - 1, 0) * inside
        coefs[level, 1] = pltpu.roll(smoothing - 0.5 * east, 1, 0) * inside
        coefs[level, 2] = pltpu.roll(smoothing + 0.5 * north, lanes - 1, 1) * inside
        coefs[level, 3] = pltpu.roll(smoothing - 0.5 * north, 1, 1) * inside

    scored = jnp.where(measure_step[0] == steps, 1.0, 0.0) * mask
    for row in range(levels * groups):
        begin = scored * tables[0][row]
        adjoint[row, 0:tiles] = begin
        adjoint[row, tiles : 2 * tiles] = begin
    steps_back(
        dims, rows, measure_step, steps - 1, count, mask, light, tables, wide, adjoint, coefs, sums, solving, lit
    )


def late_kernel(dims, rows, count, parts, out_rows, measure_step, *refs):
    pieces, refs = refs[:parts], refs[parts:]
    tables, refs = refs[:5], refs[5:]
    given, coefs, early_sums, cells, out, wide, adjoint, sums, solving, lit = refs
    steps, groups, part, tiles, own, halo = dims
    levels = adjoint.shape[0] // groups
    fields = groups * quads
    cell = (tiles, lanes)
    widen(dims, rows, pieces, wide)
    adjoint[...] = given[...]
    steps_back(
        dims,
        rows,
        measure_step,
        count - 1,
        count,
        cells[0],
        cells[1],
        tables,
        wide,
        adjoint,
        coefs,
        sums,
        solving,
        lit,
    )

    stack = tiles // quads
    short = levels // stack
    home = (lane_iota(cell) % window) // own
    for group in range(groups):
        for level in range(short):
            whole = jnp.zeros(cell, jnp.float32)
            for high in range(stack):
                value = adjoint[(high * short + level) * groups + group, 0:tiles]
                turned = pltpu.roll(value, (high * own - halo) % lanes, 1)
                whole = jnp.where(home == high, turned, whole)
            out[pl.ds(group * short + level, tiles, stride=out_rows), :] = whole
    shape = (8, lanes)
    chosen = jnp.where(lax.broadcasted_iota(jnp.int32, shape, 0) == lane_iota(shape) // window, 1.0, 0.0)
    base = groups * short
    gap = jnp.zeros((quads, lanes // 2 - levels), jnp.float32)
    for back in range(count):
        for group in range(groups):
            pair = []
            for table in (early_sums, sums):
                pair.append(
                    lax.dot_general(
                        chosen,
                        table[pl.ds(back * levels * groups + group, levels, stride=groups), :],
                        (((1,), (1,)), ((), ())),
                        precision=exact,
                        preferred_element_type=jnp.float32,
                    )[:quads]
                )
            line = jnp.concatenate([pair[0], gap, pair[1], gap], axis=1)
            for longitude in range(tiles):
                at = longitude * out_rows + base + back * fields + group * quads
                out[at : at + quads, :] = line
    for longitude in range(tiles):
        at = longitude * out_rows + base + count * fields
        if at < (longitude + 1) * out_rows:
            rest = (longitude + 1) * out_rows - at
            out[at : at + rest, :] = jnp.zeros((rest, lanes), jnp.float32)


def unpack_kernel(dims, arrived, state_adjoint, driver_grad):
    steps, groups, levels, fields, tiles, own, cells = dims
    stack = tiles // quads
    short = levels // stack
    base = groups * short
    half = steps // 2
    values = [arrived[tile, 0:base, :] for tile in range(tiles)]
    home = lane_iota((base, lanes)) // own
    apart = 1
    while apart < tiles:
        for low in range(tiles):
            if low & apart:
                continue
            first, second = values[low], values[low + apart]
            here = (home & apart) == 0
            values[low] = jnp.where(here, first, pltpu.roll(second, apart * own, 1))
            values[low + apart] = jnp.where(here, pltpu.roll(first, lanes - apart * own, 1), second)
        apart *= 2
    for high in range(stack):
        for quad in range(quads):
            for group in range(groups):
                at = (group * quads + quad) * levels + high * short
                state_adjoint[at : at + short, :] = values[quad * stack + high][group * short : (group + 1) * short]
    total = arrived[0, base : base + half * fields, :]
    for tile in range(1, tiles):
        total = total + arrived[tile, base : base + half * fields, :]
    total = total / cells
    late = pltpu.roll(total, lanes // 2, 1)
    for back in range(half):
        at = (steps - 1 - back) * fields
        driver_grad[at : at + fields, :] = total[back * fields : (back + 1) * fields, :levels]
        at = (half - 1 - back) * fields
        driver_grad[at : at + fields, :] = late[back * fields : (back + 1) * fields, :levels]


def across(value, bit):
    count = lax.axis_size("obj")
    return lax.ppermute(value, "obj", [(place, place ^ bit) for place in range(count)])


def gathered(mine):
    pieces = {0: mine}
    bits = []
    bit = 1
    while bit < lax.axis_size("obj"):
        bits.append(bit)
        bit *= 2
    for bit in bits[1:] + bits[:1]:
        for apart in sorted(pieces):
            pieces[apart ^ bit] = across(pieces[apart], bit)
    return [pieces[apart] for apart in range(len(pieces))]


def cost(micros):
    return pl.CostEstimate(flops=0, bytes_accessed=int(micros * 3_000_000), transcendentals=0)


def per_device(
    checkpoints,
    courant,
    insolation,
    region_mask,
    measure_step,
    snr_weight,
    diffusion_number,
    coupling,
    recombination,
):
    steps, fields, part = checkpoints.shape[:3]
    levels = snr_weight.shape[1]
    tiles = lax.axis_size("tile")
    parts = levels // part
    groups = fields // quads
    own = lanes // tiles
    halo = (window - own) // 2
    count = steps // 2
    dims = (steps, groups, part, tiles, own, halo)
    spots = {"wind": count * groups * part}
    spots["cells"] = spots["wind"] + part
    rows = (up(spots["cells"] + 1, 16), up((steps - count) * groups * part, 16))
    short = levels // (tiles // quads)
    out_rows = up(groups * short + count * fields, 8)
    limit = pltpu.CompilerParams(vmem_limit_bytes=48 * 2**20)
    in_vmem = pl.BlockSpec(memory_space=pltpu.VMEM)
    in_smem = pl.BlockSpec(memory_space=pltpu.SMEM)
    f32 = jnp.float32
    cell = (tiles, lanes)
    full = (levels * groups,) + cell

    packed = pl.pallas_call(
        functools.partial(pack_kernel, dims, rows, spots),
        out_shape=jax.ShapeDtypeStruct((tiles, sum(rows), lanes), jnp.bfloat16),
        in_specs=[in_vmem] * 4,
        out_specs=in_vmem,
        scratch_shapes=[pltpu.VMEM((quads, sum(rows), lanes), f32)],
        compiler_params=limit,
        cost_estimate=cost(1),
    )(
        checkpoints.reshape(steps, fields, part, lanes),
        courant.reshape(2, levels, lanes),
        insolation,
        region_mask.reshape(1, lanes),
    )
    strips = lax.all_to_all(packed, "tile", 0, 0, tiled=True)
    early = gathered(strips[:, : rows[0]])
    late = gathered(strips[:, rows[0] :])

    tables = pl.pallas_call(
        functools.partial(prepare_kernel, tiles),
        out_shape=(
            jax.ShapeDtypeStruct(full, f32),
            jax.ShapeDtypeStruct(((levels + 1) * groups,) + cell, f32),
            jax.ShapeDtypeStruct(full, f32),
            jax.ShapeDtypeStruct((groups * groups * quads,) + cell, f32),
            jax.ShapeDtypeStruct((groups,) + cell, f32),
        ),
        in_specs=[in_vmem] * 4,
        out_specs=(in_vmem,) * 5,
        scratch_shapes=[pltpu.VMEM((levels * 8, lanes), f32), pltpu.VMEM((levels * 8, lanes), f32)],
        compiler_params=limit,
        cost_estimate=cost(2),
    )(snr_weight, diffusion_number, coupling, recombination.reshape(fields, 1))

    work = [pltpu.VMEM(full, f32), pltpu.VMEM((levels * groups * tiles, lanes), f32)]
    known = pl.pallas_call(
        functools.partial(early_kernel, dims, rows[0], spots, count, parts),
        out_shape=(
            jax.ShapeDtypeStruct((levels * groups, 2 * tiles, lanes), f32),
            jax.ShapeDtypeStruct((levels, 4) + cell, f32),
            jax.ShapeDtypeStruct((count * groups * levels, lanes), f32),
            jax.ShapeDtypeStruct((2,) + cell, f32),
        ),
        in_specs=[in_smem] + [in_vmem] * (parts + 5),
        out_specs=(in_vmem,) * 4,
        scratch_shapes=[pltpu.VMEM((parts * tiles * rows[0], lanes), f32)] + work,
        compiler_params=limit,
        cost_estimate=cost(5),
    )(measure_step, *early, *tables)

    result = pl.pallas_call(
        functools.partial(late_kernel, dims, rows[1], steps - count, parts, out_rows),
        out_shape=jax.ShapeDtypeStruct((tiles * out_rows, lanes), f32),
        in_specs=[in_smem] + [in_vmem] * (parts + 9),
        out_specs=in_vmem,
        scratch_shapes=[
            pltpu.VMEM((parts * tiles * rows[1], lanes), f32),
            pltpu.VMEM((levels * groups, 2 * tiles, lanes), f32),
            pltpu.VMEM(((steps - count) * groups * levels, lanes), f32),
        ]
        + work,
        compiler_params=limit,
        cost_estimate=cost(5),
    )(measure_step, *late, *tables, *known)
    home = lax.all_to_all(result.reshape(tiles, out_rows, lanes), "tile", 0, 0, tiled=True)

    state_adjoint, driver_grad = pl.pallas_call(
        functools.partial(unpack_kernel, (steps, groups, levels, fields, tiles, own, tiles * lanes)),
        out_shape=(
            jax.ShapeDtypeStruct((fields * levels, lanes), f32),
            jax.ShapeDtypeStruct((steps * fields, levels), f32),
        ),
        in_specs=[in_vmem],
        out_specs=(in_vmem, in_vmem),
        compiler_params=limit,
    )(home)
    return (state_adjoint.reshape(1, fields, levels, 1, lanes), driver_grad.reshape(1, steps, fields, levels))


def solution(mesh):
    return jax.shard_map(
        per_device,
        mesh=mesh,
        in_specs=(
            P(None, None, "obj", "tile", None),
            P(None, None, "tile", None),
            P("tile", None),
            P("obj", "tile", None),
            P("obj"),
            P(),
            P(),
            P(),
            P(),
        ),
        out_specs=(P("obj", None, None, "tile", None), P("obj", None, None, None)),
        check_vma=False,
    )
```

time: 100 us -> 71.5 us (0.71)
  between operations: 14.7 us -> 1.41 us
  waiting for transfers between devices: 20.3 us -> 9.22 us
  Pallas kernels: 19.7 us -> 15.6 us
  starting transfers between devices: 0.04 us -> 2.67 us
  local copies, waits for them, and re-layouts: 5.37 us -> 3.22 us
    all_gather x1 -> x0, waiting for transfers between devices: 20.3 us -> none  [per_device(): arrived = lax.all_gather(strips, 'obj', axis=0, tiled=False)]
    ppermute x0 -> x6, waiting for transfers between devices: none -> 9.22 us  [across(): lax.ppermute(value, 'obj', [(place, place ^ bit) for place in range(count)])]
    pallas_call x2 -> x4, Pallas kernels: 18.7 us -> 14.6 us  [the longest x1 7.23 us: per_device(): pl.pallas_call(functools.partial(early_kernel, dims, rows[0], spots, coun...]
    ppermute x0 -> x6, starting transfers between devices: none -> 2.67 us  [across(): lax.ppermute(value, 'obj', [(place, place ^ bit) for place in range(count)])]
    unnamed x19 -> x16, local copies, waits for them, and re-layouts: 5.27 us -> 3.09 us
  transfers between devices with their start and end apart: 1 -> 6, of which waited for: 1 -> 2; matrix products, arithmetic and copies ran while one was open for 0% -> 0% of each run, Pallas kernels for 0% -> 11%
where the time goes in v2:
time: 71.5 us; the launch traced here: 71.2 us
  blocking collectives  39 us (55%)
  Pallas kernels  15.6 us (22%)
  waiting for transfers between devices  9.22 us (13%)
  local copies, waits for them, and re-layouts  3.22 us (5%)
  starting transfers between devices  2.67 us (4%)
  between operations  1.41 us (2%)
    all_to_all x1, blocking collectives, per_device(): strips = lax.all_to_all(packed, 'tile', 0, 0, tiled=True)  21 us
    all_to_all x1, blocking collectives, per_device(): lax.all_to_all(result.reshape(tiles, out_rows, lanes), 'tile', 0, 0, tile...  18 us
    ppermute x6, waiting for transfers between devices, across(): lax.ppermute(value, 'obj', [(place, place ^ bit) for place in range(count)])  9.22 us
    pallas_call x1, Pallas kernels, per_device(): pl.pallas_call(functools.partial(early_kernel, dims, rows[0], spots, coun...  7.23 us
    pallas_call x1, Pallas kernels, per_device(): pl.pallas_call(functools.partial(late_kernel, dims, rows[1], steps - coun...  6.1 us
    unnamed x16, local copies, waits for them, and re-layouts  3.09 us
    ppermute x6, starting transfers between devices, across(): lax.ppermute(value, 'obj', [(place, place ^ bit) for place in range(count)])  2.67 us
  transfers between devices with their start and end apart: 6, of which 2 were waited for; matrix products, arithmetic and copies ran while one was open for 0% of the time, Pallas kernels for 11%

profile of v2, /device:TPU:0, one launch (start us, length us, event | category | flops | bytes accessed | tf_op | source)
XLA Modules:
  0.0 71.2 jit_solution(17192850938100522083)
XLA Ops:
  0.6 0.0 copy-start
  0.6 1.0 %copy-done = bf16[6,12,12,1,128]{4,2,3,1,0:T(8,128)(2,1)S(1)} copy-done((bf16[6,12,12,1,128]{4,2,3,1,0:T(8,128)(2,1)S(1)}, bf16[6,12,12,1,128]{4,2,3,1,0:T(8,128)(2,1)}, u32[]{:S(2)}) %copy-start) | copy-done | bytes 221208
  1.6 0.0 copy-start.1
  1.6 0.8 %copy-done.1 = f32[2,48,1,128]{3,2,1,0:T(1,128)S(1)} copy-done((f32[2,48,1,128]{3,2,1,0:T(1,128)S(1)}, f32[2,48,1,128]{3,2,1,0:T(1,128)}, u32[]{:S(2)}) %copy-start.1) | copy-done | bytes 49176
  2.4 0.0 copy-start.5
  2.4 0.7 copy-done.5
  3.0 0.0 copy-start.6
  3.0 0.7 copy-done.6
  3.7 0.7 shard_map.104
  4.4 0.0 copy-start.7
  4.4 0.0 copy-start.2
  4.4 0.0 copy-start.3
  4.4 0.0 copy-start.4
  4.4 21.0 %all_to_all.10 = bf16[8,240,128]{2,1,0:T(8,128)(2,1)S(1)} all-to-all(bf16[8,240,128]{2,1,0:T(8,128)(2,1)S(1)} %shard_map.104), channel_id=1, replica_groups=mesh['obj'=4,'tile'=8] {'tile'}, dimensions={0} | all-to-all | bytes 983040 | tf_op jit(solution)/shard_map/all_to_all | solution.py:439
  25.5 1.6 %collective-permute-start.4 = (bf16[8,128,128]{2,1,0:T(8,128)(2,1)S(1)}, bf16[8,128,128]{2,1,0:T(8,128)(2,1)S(1)}, u32[]{:S(2)}, u32[]{:S(2)}) collective-permute-start(bf16[8,128,128]{2,1,0:T(8,128)(2,1)S(1)} %slice.9.refs_0_), channel_id=1, source_target_pairs={{0,16},{8,24},{16,0},{24,8},{1,17},{9,25},{17,1},{25,9},{2,18},{10... | collective-permute-start | bytes 786440 | tf_op jit(solution)/shard_map/ppermute | solution.py:373
  27.1 0.6 collective-permute-start.1
  27.7 0.0 collective-permute-start.3
  27.7 7.1 %collective-permute-done.4.refs_2_ = bf16[8,128,128]{2,1,0:T(8,128)(2,1)S(1)} collective-permute-done((bf16[8,128,128]{2,1,0:T(8,128)(2,1)S(1)}, bf16[8,128,128]{2,1,0:T(8,128)(2,1)S(1)}, u32[]{:S(2)}, u32[]{:S(2)}) %collective-permute-start.4) | collective-permute-done | bytes 262176 | tf_op jit(solution)/shard_map/ppermute | solution.py:373
  34.8 0.0 collective-permute-start.5
  34.8 0.5 collective-permute-start
  35.3 2.1 %collective-permute-done.1.refs_2_ = bf16[8,112,128]{2,1,0:T(8,128)(2,1)S(1)} collective-permute-done((bf16[8,112,128]{2,1,0:T(8,128)(2,1)S(1)}, bf16[8,112,128]{2,1,0:T(8,128)(2,1)S(1)}, u32[]{:S(2)}, u32[]{:S(2)}) %collective-permute-start.1) | collective-permute-done | bytes 229408 | tf_op jit(solution)/shard_map/ppermute | solution.py:373
  37.4 0.0 collective-permute-start.2
  37.4 0.0 copy-done.7
  37.4 0.1 copy.14.recombination
  38.2 0.0 copy-done.2
  38.2 0.0 copy-done.3
  38.2 0.0 copy-done.4
  38.2 0.5 shard_map.105
  38.7 0.0 collective-permute-done.3.refs_1_
  38.7 0.0 collective-permute-done.5.refs_3_
  38.8 7.2 %shard_map.106 = (f32[144,16,128]{2,1,0:T(8,128)S(1)}, f32[48,4,8,128]{3,2,1,0:T(8,128)S(1)}, f32[432,128]{1,0:T(8,128)S(1)}, f32[2,8,128]{2,1,0:T(8,128)S(1)}) custom-call(s32[1]{0:T(128)S(6)} %copy.17.measure_step, bf16[8,128,128]{2,1,0:T(8,128)(2,1)S(1)} %slice.9.refs_0_, bf16[8,128,128]{2,1,0:T(8,128)(2,1)S(1)} %collective-permute-done.3.refs_1_, ...), custom_call_target="tpu_custom_call" | custom-call | bytes 15000000 | tf_op jit(solution)/shard_map/pallas_call | solution.py:460
  46.0 0.0 collective-permute-done.refs_1_
  46.0 0.0 collective-permute-done.2.refs_3_
  46.0 6.1 %shard_map.107 = f32[896,128]{1,0:T(8,128)S(1)} custom-call(s32[1]{0:T(128)S(6)} %copy.17.measure_step, bf16[8,112,128]{2,1,0:T(8,128)(2,1)S(1)} %slice.8.refs_0_, bf16[8,112,128]{2,1,0:T(8,128)(2,1)S(1)} %collective-permute-done.refs_1_, bf16[8,112,128]{2,1,0:T(8,128)(2,1)S(1)} %collective-permute-done.1.refs_2_, ...), custom_call_target="tpu_custom_call" | custom-call | bytes 15000000 | tf_op jit(solution)/shard_map/pallas_call | solution.py:475
  52.1 18.0 %all_to_all.11.arrived = f32[8,112,128]{2,1,0:T(8,128)S(1)} all-to-all(f32[8,112,128]{2,1,0:T(8,128)S(1)} %bitcast.9), channel_id=1, replica_groups=mesh['obj'=4,'tile'=8] {'tile'}, dimensions={0} | all-to-all | bytes 917504 | tf_op jit(solution)/shard_map/all_to_all | solution.py:489
  70.1 1.1 %shard_map.108 = (f32[576,128]{1,0:T(8,128)}, f32[72,48]{1,0:T(8,128)}) custom-call(f32[8,112,128]{2,1,0:T(8,128)S(1)} %all_to_all.11.arrived), custom_call_target="tpu_custom_call" | custom-call | tf_op jit(solution)/shard_map/pallas_call | solution.py:491
  (2 shorter events, 0.0 us)
Async XLA Ops:
  0.6 1.0 %copy-start = (bf16[6,12,12,1,128]{4,2,3,1,0:T(8,128)(2,1)S(1)}, bf16[6,12,12,1,128]{4,2,3,1,0:T(8,128)(2,1)}, u32[]{:S(2)}) copy-start(bf16[6,12,12,1,128]{4,2,3,1,0:T(8,128)(2,1)} %param.9) | copy-start | bytes 663556
  1.6 0.8 %copy-start.1 = (f32[2,48,1,128]{3,2,1,0:T(1,128)S(1)}, f32[2,48,1,128]{3,2,1,0:T(1,128)}, u32[]{:S(2)}) copy-start(f32[2,48,1,128]{3,2,1,0:T(1,128)} %param.10) | copy-start | bytes 147460
  2.4 0.7 copy-start.5
  3.0 0.7 copy-start.6
  4.4 33.0 %copy-start.7 = (f32[12]{0:T(128)S(1)}, f32[12]{0:T(128)}, u32[]{:S(2)}) copy-start(f32[12]{0:T(128)} %param.17) | copy-start | bytes 148
  4.4 33.8 %copy-start.2 = (f32[12,48]{1,0:T(8,128)S(1)}, f32[12,48]{1,0:T(8,128)}, u32[]{:S(2)}) copy-start(f32[12,48]{1,0:T(8,128)} %snr_weight.1) | copy-start | bytes 6916
  4.4 33.8 %copy-start.3 = (f32[12,47]{1,0:T(8,128)S(1)}, f32[12,47]{1,0:T(8,128)}, u32[]{:S(2)}) copy-start(f32[12,47]{1,0:T(8,128)} %diffusion.1) | copy-start | bytes 6772
  4.4 33.8 %copy-start.4 = (f32[12,12]{1,0:T(8,128)S(1)}, f32[12,12]{1,0:T(8,128)}, u32[]{:S(2)}) copy-start(f32[12,12]{1,0:T(8,128)} %coupling.1) | copy-start | bytes 1732
  25.5 9.3 %collective-permute-start.4 = (bf16[8,128,128]{2,1,0:T(8,128)(2,1)S(1)}, bf16[8,128,128]{2,1,0:T(8,128)(2,1)S(1)}, u32[]{:S(2)}, u32[]{:S(2)}) collective-permute-start(bf16[8,128,128]{2,1,0:T(8,128)(2,1)S(1)} %slice.9.refs_0_), channel_id=1, source_target_pairs={{0,16},{8,24},{16,0},{24,8},{1,17},{9,25},{17,1},{25,9},{2,18},{10... | collective-permute-start | bytes 786440 | tf_op jit(solution)/shard_map/ppermute | solution.py:373
  27.1 10.3 %collective-permute-start.1 = (bf16[8,112,128]{2,1,0:T(8,128)(2,1)S(1)}, bf16[8,112,128]{2,1,0:T(8,128)(2,1)S(1)}, u32[]{:S(2)}, u32[]{:S(2)}) collective-permute-start(bf16[8,112,128]{2,1,0:T(8,128)(2,1)S(1)} %slice.8.refs_0_), channel_id=1, source_target_pairs={{0,16},{8,24},{16,0},{24,8},{1,17},{9,25},{17,1},{25,9},{2,18},{10... | collective-permute-start | bytes 688136 | tf_op jit(solution)/shard_map/ppermute | solution.py:373
  27.7 11.1 %collective-permute-start.3 = (bf16[8,128,128]{2,1,0:T(8,128)(2,1)S(1)}, bf16[8,128,128]{2,1,0:T(8,128)(2,1)S(1)}, u32[]{:S(2)}, u32[]{:S(2)}) collective-permute-start(bf16[8,128,128]{2,1,0:T(8,128)(2,1)S(1)} %slice.9.refs_0_), channel_id=1, source_target_pairs={{0,8},{8,0},{16,24},{24,16},{1,9},{9,1},{17,25},{25,17},{2,10},{10... | collective-permute-start | bytes 786440 | tf_op jit(solution)/shard_map/ppermute | solution.py:373
  34.8 3.9 %collective-permute-start.5 = (bf16[8,128,128]{2,1,0:T(8,128)(2,1)S(1)}, bf16[8,128,128]{2,1,0:T(8,128)(2,1)S(1)}, u32[]{:S(2)}, u32[]{:S(2)}) collective-permute-start(bf16[8,128,128]{2,1,0:T(8,128)(2,1)S(1)} %collective-permute-done.4.refs_2_), channel_id=1, source_target_pairs={{0,8},{8,0},{16,24},{24,16},{1,9},{9,1},{17,25},{25,17},{2,10},{10... | collective-permute-start | bytes 786440 | tf_op jit(solution)/shard_map/ppermute | solution.py:373
  34.8 11.2 %collective-permute-start = (bf16[8,112,128]{2,1,0:T(8,128)(2,1)S(1)}, bf16[8,112,128]{2,1,0:T(8,128)(2,1)S(1)}, u32[]{:S(2)}, u32[]{:S(2)}) collective-permute-start(bf16[8,112,128]{2,1,0:T(8,128)(2,1)S(1)} %slice.8.refs_0_), channel_id=1, source_target_pairs={{0,8},{8,0},{16,24},{24,16},{1,9},{9,1},{17,25},{25,17},{2,10},{10... | collective-permute-start | bytes 688136 | tf_op jit(solution)/shard_map/ppermute | solution.py:373
  37.4 8.6 %collective-permute-start.2 = (bf16[8,112,128]{2,1,0:T(8,128)(2,1)S(1)}, bf16[8,112,128]{2,1,0:T(8,128)(2,1)S(1)}, u32[]{:S(2)}, u32[]{:S(2)}) collective-permute-start(bf16[8,112,128]{2,1,0:T(8,128)(2,1)S(1)} %collective-permute-done.1.refs_2_), channel_id=1, source_target_pairs={{0,8},{8,0},{16,24},{24,16},{1,9},{9,1},{17,25},{25,17},{2,10},{10... | collective-permute-start | bytes 688136 | tf_op jit(solution)/shard_map/ppermute | solution.py:373

commit v3 on v2

--- a/solution.py
+++ b/solution.py
@@ -12,6 +12,7 @@
 quads = 4
 window = lanes // quads
 exact = lax.Precision.HIGHEST
+early_steps = 2
 
 
 def up(value, unit):
@@ -22,9 +23,16 @@
     return lax.broadcasted_iota(jnp.int32, shape, len(shape) - 1)
 
 
-def pack_kernel(dims, rows, spots, checkpoints, courant, insolation, region_mask, out, staged):
+def pack_kernel(dims, rows, spots, *refs):
+    outside, out, staged, inside, arrival = refs[:4], refs[4], refs[5], refs[6:10], refs[10]
+    copies = [pltpu.make_async_copy(outside[i], inside[i], arrival.at[i]) for i in range(4)]
+    for copy in copies:
+        copy.start()
+    for copy in copies:
+        copy.wait()
+    checkpoints, courant, insolation, region_mask = inside
     steps, groups, part, tiles, own, halo = dims
-    count = steps // 2
+    count = early_steps
     ours = lax.axis_index("obj") * part
     total = sum(rows)
     for quad in range(quads):
@@ -150,7 +158,8 @@
     latitude = own * lax.axis_index("tile") - halo + lane_iota(cell) % window
     inside = jnp.where((latitude >= 0) & (latitude < lanes), 1.0, 0.0)
     centre = (1.0 - 4.0 * smoothing) * inside
-    block = 12 if levels % 12 == 0 else 2
+    block = 12 if levels % 12 == 0 else levels
+    together = 3 if block % 3 == 0 else 1
     nothing = tuple(jnp.zeros(cell, jnp.float32) for _ in range(groups))
 
     def step(back, carry):
@@ -162,14 +171,15 @@
             before = list(before)
             for inner in range(block):
                 level = at * block + inner
+                weight = [coefs[level, way] for way in range(4)]
                 for group in range(groups):
                     row = level * groups + group
                     value = adjoint[row, 0:tiles]
                     moved = centre * value
-                    moved = moved + coefs[level, 0] * adjoint[row, 1 : tiles + 1]
-                    moved = moved + coefs[level, 1] * adjoint[row, tiles - 1 : 2 * tiles - 1]
-                    moved = moved + coefs[level, 2] * pltpu.roll(value, lanes - 1, 1)
-                    moved = moved + coefs[level, 3] * pltpu.roll(value, 1, 1)
+                    moved = moved + weight[0] * adjoint[row, 1 : tiles + 1]
+                    moved = moved + weight[1] * adjoint[row, tiles - 1 : 2 * tiles - 1]
+                    moved = moved + weight[2] * pltpu.roll(value, lanes - 1, 1)
+                    moved = moved + weight[3] * pltpu.roll(value, 1, 1)
                     moved = moved + multiplier[row] * before[group]
                     before[group] = moved
                     solving[row] = moved * inverse[row]
@@ -179,8 +189,8 @@
 
         def backward(at, after):
             after = list(after)
-            for inner in range(0, block, 2):
-                pair = [levels - 1 - (at * block + inner), levels - 2 - (at * block + inner)]
+            for inner in range(0, block, together):
+                pair = [levels - 1 - (at * block + inner + more) for more in range(together)]
                 turned = []
                 states = []
                 for level in pair:
@@ -200,14 +210,14 @@
                     result = [
                         loss[group] * states[at_pair][group] * turned[at_pair][group][0]
                         + scored * snr[pair[at_pair] * groups + group]
-                        for at_pair in range(2)
+                        for at_pair in range(together)
                     ]
                     for source in range(groups):
                         for turn in range(quads):
                             factor = mixing[(group * groups + source) * quads + turn]
-                            for at_pair in range(2):
+                            for at_pair in range(together):
                                 result[at_pair] = result[at_pair] + factor * turned[at_pair][source][turn]
-                    for at_pair in range(2):
+                    for at_pair in range(together):
                         row = pair[at_pair] * groups + group
                         adjoint[row, 0:tiles] = result[at_pair]
                         adjoint[row, tiles : 2 * tiles] = result[at_pair]
@@ -309,25 +319,27 @@
     chosen = jnp.where(lax.broadcasted_iota(jnp.int32, shape, 0) == lane_iota(shape) // window, 1.0, 0.0)
     base = groups * short
     gap = jnp.zeros((quads, lanes // 2 - levels), jnp.float32)
-    for back in range(count):
+    half = steps // 2
+
+    def summed(back, group):
+        early = steps - count
+        table, place = (early_sums, back) if back < early else (sums, back - early)
+        return lax.dot_general(
+            chosen,
+            table[pl.ds(place * levels * groups + group, levels, stride=groups), :],
+            (((1,), (1,)), ((), ())),
+            precision=exact,
+            preferred_element_type=jnp.float32,
+        )[:quads]
+
+    for back in range(half):
         for group in range(groups):
-            pair = []
-            for table in (early_sums, sums):
-                pair.append(
-                    lax.dot_general(
-                        chosen,
-                        table[pl.ds(back * levels * groups + group, levels, stride=groups), :],
-                        (((1,), (1,)), ((), ())),
-                        precision=exact,
-                        preferred_element_type=jnp.float32,
-                    )[:quads]
-                )
-            line = jnp.concatenate([pair[0], gap, pair[1], gap], axis=1)
+            line = jnp.concatenate([summed(back, group), gap, summed(back + half, group), gap], axis=1)
             for longitude in range(tiles):
                 at = longitude * out_rows + base + back * fields + group * quads
                 out[at : at + quads, :] = line
     for longitude in range(tiles):
-        at = longitude * out_rows + base + count * fields
+        at = longitude * out_rows + base + half * fields
         if at < (longitude + 1) * out_rows:
             rest = (longitude + 1) * out_rows - at
             out[at : at + rest, :] = jnp.zeros((rest, lanes), jnp.float32)
@@ -373,16 +385,34 @@
     return lax.ppermute(value, "obj", [(place, place ^ bit) for place in range(count)])
 
 
-def gathered(mine):
+def hold(value, *after):
+    def nothing(*refs):
+        pass
+
+    anywhere = pl.BlockSpec(memory_space=pl.ANY)
+    return pl.pallas_call(
+        nothing,
+        out_shape=jax.ShapeDtypeStruct(value.shape, value.dtype),
+        in_specs=[anywhere] * (1 + len(after)),
+        out_specs=anywhere,
+        input_output_aliases={0: 0},
+    )(value, *after)
+
+
+def over_chips(mine):
     pieces = {0: mine}
-    bits = []
-    bit = 1
+    bit = 2
     while bit < lax.axis_size("obj"):
-        bits.append(bit)
-        bit *= 2
-    for bit in bits[1:] + bits[:1]:
         for apart in sorted(pieces):
             pieces[apart ^ bit] = across(pieces[apart], bit)
+        bit *= 2
+    return pieces
+
+
+def over_cores(pieces):
+    if lax.axis_size("obj") > 1:
+        for apart in sorted(pieces):
+            pieces[apart ^ 1] = across(pieces[apart], 1)
     return [pieces[apart] for apart in range(len(pieces))]
 
 
@@ -408,13 +438,13 @@
     groups = fields // quads
     own = lanes // tiles
     halo = (window - own) // 2
-    count = steps // 2
+    count = early_steps
     dims = (steps, groups, part, tiles, own, halo)
     spots = {"wind": count * groups * part}
     spots["cells"] = spots["wind"] + part
-    rows = (up(spots["cells"] + 1, 16), up((steps - count) * groups * part, 16))
+    rows = (up(spots["cells"] + 1, 8), up((steps - count) * groups * part, 8))
     short = levels // (tiles // quads)
-    out_rows = up(groups * short + count * fields, 8)
+    out_rows = up(groups * short + steps // 2 * fields, 8)
     limit = pltpu.CompilerParams(vmem_limit_bytes=48 * 2**20)
     in_vmem = pl.BlockSpec(memory_space=pltpu.VMEM)
     in_smem = pl.BlockSpec(memory_space=pltpu.SMEM)
@@ -425,10 +455,17 @@
     packed = pl.pallas_call(
         functools.partial(pack_kernel, dims, rows, spots),
         out_shape=jax.ShapeDtypeStruct((tiles, sum(rows), lanes), jnp.bfloat16),
-        in_specs=[in_vmem] * 4,
+        in_specs=[pl.BlockSpec(memory_space=pltpu.HBM)] * 4,
         out_specs=in_vmem,
-        scratch_shapes=[pltpu.VMEM((quads, sum(rows), lanes), f32)],
-        compiler_params=limit,
+        scratch_shapes=[
+            pltpu.VMEM((quads, sum(rows), lanes), f32),
+            pltpu.VMEM((steps, fields, part, lanes), checkpoints.dtype),
+            pltpu.VMEM((2, levels, lanes), f32),
+            pltpu.VMEM((1, lanes), f32),
+            pltpu.VMEM((1, lanes), jnp.int32),
+            pltpu.SemaphoreType.DMA((4,)),
+        ],
+        compiler_params=pltpu.CompilerParams(vmem_limit_bytes=64 * 2**20),
         cost_estimate=cost(1),
     )(
         checkpoints.reshape(steps, fields, part, lanes),
@@ -436,10 +473,6 @@
         insolation,
         region_mask.reshape(1, lanes),
     )
-    strips = lax.all_to_all(packed, "tile", 0, 0, tiled=True)
-    early = gathered(strips[:, : rows[0]])
-    late = gathered(strips[:, rows[0] :])
-
     tables = pl.pallas_call(
         functools.partial(prepare_kernel, tiles),
         out_shape=(
@@ -456,6 +489,11 @@
         cost_estimate=cost(2),
     )(snr_weight, diffusion_number, coupling, recombination.reshape(fields, 1))
 
+    strips = lax.all_to_all(packed, "tile", 0, 0, tiled=True)
+    early = over_chips(strips[:, : rows[0]])
+    late = over_chips(hold(strips[:, rows[0] :], *[early[apart] for apart in sorted(early)[1:]], tables[4]))
+    early = over_cores(early)
+
     work = [pltpu.VMEM(full, f32), pltpu.VMEM((levels * groups * tiles, lanes), f32)]
     known = pl.pallas_call(
         functools.partial(early_kernel, dims, rows[0], spots, count, parts),
@@ -472,6 +510,7 @@
         cost_estimate=cost(5),
     )(measure_step, *early, *tables)
 
+    late = over_cores({apart: hold(late[apart], known[3]) if apart else late[apart] for apart in late})
     result = pl.pallas_call(
         functools.partial(late_kernel, dims, rows[1], steps - count, parts, out_rows),
         out_shape=jax.ShapeDtypeStruct((tiles * out_rows, lanes), f32),

time: 71.5 us -> 76.6 us (1.071)
  local copies, waits for them, and re-layouts: 3.22 us -> 9.88 us
  waiting for transfers between devices: 9.22 us -> 4.76 us
  Pallas kernels: 15.6 us -> 17.7 us
  starting transfers between devices: 2.67 us -> 3.89 us
    unnamed x16 -> x38, local copies, waits for them, and re-layouts: 3.09 us -> 9.02 us
    ppermute x6, waiting for transfers between devices: 9.22 us -> 4.76 us  [across(): lax.ppermute(value, 'obj', [(place, place ^ bit) for place in range(count)])]
    pallas_call x1, Pallas kernels: 6.1 us -> 8.64 us  [per_device(): pl.pallas_call(functools.partial(late_kernel, dims, rows[1], steps - coun...]
    pallas_call x1, Pallas kernels: 7.23 us -> 5.01 us  [per_device(): pl.pallas_call(functools.partial(early_kernel, dims, rows[0], spots, coun...]
    pallas_call x1, Pallas kernels: 0.69 us -> 2.48 us  [per_device(): pl.pallas_call(functools.partial(pack_kernel, dims, rows, spots), out_sha...]
    ppermute x6, starting transfers between devices: 2.67 us -> 3.89 us  [across(): lax.ppermute(value, 'obj', [(place, place ^ bit) for place in range(count)])]
  transfers between devices with their start and end apart: 6 -> 6, of which waited for: 2 -> 4; matrix products, arithmetic and copies ran while one was open for 0% -> 1% of each run, Pallas kernels for 11% -> 7%
where the time goes in v3:
time: 76.6 us; the launch traced here: 76.1 us
  blocking collectives  38.4 us (50%)
  Pallas kernels  17.7 us (23%)
  local copies, waits for them, and re-layouts  9.88 us (13%)
  waiting for transfers between devices  4.76 us (6%)
  starting transfers between devices  3.89 us (5%)
  between operations  1.4 us (2%)
    all_to_all x1, blocking collectives, per_device(): strips = lax.all_to_all(packed, 'tile', 0, 0, tiled=True)  20.9 us
    all_to_all x1, blocking collectives, per_device(): lax.all_to_all(result.reshape(tiles, out_rows, lanes), 'tile', 0, 0, tile...  17.5 us
    unnamed x38, local copies, waits for them, and re-layouts  9.02 us
    pallas_call x1, Pallas kernels, per_device(): pl.pallas_call(functools.partial(late_kernel, dims, rows[1], steps - coun...  8.64 us
    pallas_call x1, Pallas kernels, per_device(): pl.pallas_call(functools.partial(early_kernel, dims, rows[0], spots, coun...  5.01 us
    ppermute x6, waiting for transfers between devices, across(): lax.ppermute(value, 'obj', [(place, place ^ bit) for place in range(count)])  4.76 us
    ppermute x6, starting transfers between devices, across(): lax.ppermute(value, 'obj', [(place, place ^ bit) for place in range(count)])  3.89 us
    pallas_call x1, Pallas kernels, per_device(): pl.pallas_call(functools.partial(pack_kernel, dims, rows, spots), out_sha...  2.48 us
  transfers between devices with their start and end apart: 6, of which 4 were waited for; matrix products, arithmetic and copies ran while one was open for 1% of the time, Pallas kernels for 7%

profile of v3, /device:TPU:0, one launch (start us, length us, event | category | flops | bytes accessed | tf_op | source)
XLA Modules:
  0.0 76.1 jit_solution(1808522201772778800)
XLA Ops:
  0.6 2.5 %shard_map.104 = bf16[8,232,128]{2,1,0:T(8,128)(2,1)} custom-call(bf16[6,12,12,128]{3,2,1,0:T(8,128)(2,1)} %bitcast.10, f32[2,48,128]{2,1,0:T(8,128)} %bitcast.11, f32[1,128]{1,0:T(1,128)} %refs_2_.1, s32[1,128]{1,0:T(1,128)} %bitcast.12), custom_call_target="tpu_custom_call" | custom-call | bytes 3000000 | tf_op jit(solution)/shard_map/pallas_call | solution.py:455
  3.1 0.0 copy-start.18
  3.1 0.0 copy-start.15
  3.1 0.0 copy-start.16
  3.2 0.0 copy-start.17
  3.2 20.9 %all_to_all.10 = bf16[8,232,128]{2,1,0:T(8,128)(2,1)S(1)} all-to-all(bf16[8,232,128]{2,1,0:T(8,128)(2,1)} %shard_map.104), channel_id=1, replica_groups=mesh['obj'=4,'tile'=8] {'tile'}, dimensions={0} | all-to-all | bytes 950272 | tf_op jit(solution)/shard_map/all_to_all | solution.py:492
  24.1 1.6 %collective-permute-start = (bf16[8,88,128]{2,1,0:T(8,128)(2,1)S(1)}, bf16[8,88,128]{2,1,0:T(8,128)(2,1)S(1)}, u32[]{:S(2)}, u32[]{:S(2)}) collective-permute-start(bf16[8,88,128]{2,1,0:T(8,128)(2,1)S(1)} %slice.9.refs_0_), channel_id=1, source_target_pairs={{0,16},{8,24},{16,0},{24,8},{1,17},{9,25},{17,1},{25,9},{2,18},{10... | collective-permute-start | bytes 540680 | tf_op jit(solution)/shard_map/ppermute | solution.py:385
  25.7 0.0 copy-done.18
  25.7 0.1 copy.16.recombination
  25.8 0.0 copy-done.15
  25.8 0.0 copy-done.16
  25.8 0.0 copy-done.17
  25.8 0.5 shard_map.105
  26.3 0.0 copy-start.10
  26.3 0.0 copy-start.5
  26.4 0.8 slice.8.refs_0_
  27.1 2.6 %collective-permute-done.refs_1_.refs_2_ = bf16[8,88,128]{2,1,0:T(8,128)(2,1)S(1)} collective-permute-done((bf16[8,88,128]{2,1,0:T(8,128)(2,1)S(1)}, bf16[8,88,128]{2,1,0:T(8,128)(2,1)S(1)}, u32[]{:S(2)}, u32[]{:S(2)}) %collective-permute-start) | collective-permute-done | bytes 180256 | tf_op jit(solution)/shard_map/ppermute | solution.py:385
  29.7 0.0 copy-start.3
  29.7 0.0 copy-done.10
  29.7 0.7 copy-done.3
  30.4 1.5 %collective-permute-start.2 = (bf16[8,144,128]{2,1,0:T(8,128)(2,1)}, bf16[8,144,128]{2,1,0:T(8,128)(2,1)}, u32[]{:S(2)}, u32[]{:S(2)}) collective-permute-start(bf16[8,144,128]{2,1,0:T(8,128)(2,1)} %shard_map.106.refs_0_), channel_id=1, source_target_pairs={{0,16},{8,24},{16,0},{24,8},{1,17},{9,25},{17,1},{25,9},{2,18},{10... | collective-permute-start | bytes 884744 | tf_op jit(solution)/shard_map/ppermute | solution.py:385
  31.9 0.0 collective-permute-start.3
  31.9 0.5 collective-permute-start.4
  33.0 0.1 collective-permute-start.1
  33.1 0.4 collective-permute-done.3.refs_1_
  33.5 0.2 collective-permute-done.4.refs_3_
  33.7 0.0 copy-done.5
  33.7 0.0 copy-start.4
  33.7 0.9 %copy-done.4 = bf16[8,88,128]{2,1,0:T(8,128)(2,1)S(1)} copy-done((bf16[8,88,128]{2,1,0:T(8,128)(2,1)S(1)}, bf16[8,88,128]{2,1,0:T(8,128)(2,1)}, u32[]{:S(2)}) %copy-start.4) | copy-done | bytes 180248
  34.7 0.0 copy-start.6
  34.7 0.9 %copy-done.6 = f32[36,8,128]{2,1,0:T(8,128)S(1)} copy-done((f32[36,8,128]{2,1,0:T(8,128)S(1)}, f32[36,8,128]{2,1,0:T(8,128)}, u32[]{:S(2)}) %copy-start.6) | copy-done | bytes 147480
  35.6 0.0 copy-start.11
  35.6 0.7 copy-done.11
  36.3 0.0 copy-start
  36.3 0.0 copy-start.12
  36.3 5.0 %shard_map.107 = (f32[144,16,128]{2,1,0:T(8,128)S(1)}, f32[48,4,8,128]{3,2,1,0:T(8,128)S(1)}, f32[288,128]{1,0:T(8,128)S(1)}, f32[2,8,128]{2,1,0:T(8,128)S(1)}) custom-call(s32[1]{0:T(128)S(6)} %copy.21.measure_step, bf16[8,88,128]{2,1,0:T(8,128)(2,1)S(1)} %slice.9.refs_0_, bf16[8,88,128]{2,1,0:T(8,128)(2,1)S(1)} %collective-permute-done.3.refs_1_, ...), custom_call_target="tpu_custom_call" | custom-call | bytes 15000000 | tf_op jit(solution)/shard_map/pallas_call | solution.py:498
  41.3 0.0 copy-start.1
  41.3 0.9 %copy-done.1 = f32[48,4,8,128]{3,2,1,0:T(8,128)} copy-done((f32[48,4,8,128]{3,2,1,0:T(8,128)}, f32[48,4,8,128]{3,2,1,0:T(8,128)S(1)}, u32[]{:S(2)}) %copy-start.1) | copy-done | bytes 786456
  42.2 0.0 copy-start.8
  42.2 0.7 copy-done.8
  42.8 0.0 copy-start.13
  42.8 0.6 copy-done.13
  43.4 0.0 collective-permute-done.2.refs_0_
  43.4 0.3 collective-permute-start.5
  43.7 0.0 collective-permute-done.1.refs_1_
  43.7 1.5 %collective-permute-done.5.refs_3_ = bf16[8,144,128]{2,1,0:T(8,128)(2,1)S(1)} collective-permute-done((bf16[8,144,128]{2,1,0:T(8,128)(2,1)}, bf16[8,144,128]{2,1,0:T(8,128)(2,1)S(1)}, u32[]{:S(2)}, u32[]{:S(2)}) %collective-permute-start.5) | collective-permute-done | bytes 294944 | tf_op jit(solution)/shard_map/ppermute | solution.py:385
  45.2 0.0 copy-done
  45.2 0.0 copy-done.12
  45.2 0.0 copy-start.2
  45.2 1.1 %copy-done.2 = f32[48,4,8,128]{3,2,1,0:T(8,128)S(1)} copy-done((f32[48,4,8,128]{3,2,1,0:T(8,128)S(1)}, f32[48,4,8,128]{3,2,1,0:T(8,128)}, u32[]{:S(2)}) %copy-start.2) | copy-done | bytes 786456
  46.4 0.0 copy-start.7
  46.4 0.9 %copy-done.7 = f32[36,8,128]{2,1,0:T(8,128)S(1)} copy-done((f32[36,8,128]{2,1,0:T(8,128)S(1)}, f32[36,8,128]{2,1,0:T(8,128)}, u32[]{:S(2)}) %copy-start.7) | copy-done | bytes 147480
  47.3 0.0 copy-start.9
  47.3 0.9 %copy-done.9 = f32[288,128]{1,0:T(8,128)S(1)} copy-done((f32[288,128]{1,0:T(8,128)S(1)}, f32[288,128]{1,0:T(8,128)}, u32[]{:S(2)}) %copy-start.9) | copy-done | bytes 147480
  48.2 0.0 copy-start.14
  48.2 0.7 copy-done.14
  48.9 8.6 %shard_map.109 = f32[896,128]{1,0:T(8,128)S(1)} custom-call(s32[1]{0:T(128)S(6)} %copy.21.measure_step, bf16[8,144,128]{2,1,0:T(8,128)(2,1)S(1)} %copy-done, bf16[8,144,128]{2,1,0:T(8,128)(2,1)} %collective-permute-done.1.refs_1_, bf16[8,144,128]{2,1,0:T(8,128)(2,1)} %shard_map.108.refs_2_, bf16[8,144,128]{2,1,0:T(8,128)(2,1)S(1)} %collective-permute-done.5.refs_3_, ...), custom_call_target="tpu_custom_call" | custom-call | bytes 15000000 | tf_op jit(solution)/shard_map/pallas_call | solution.py:514
  57.5 17.5 %all_to_all.11.arrived = f32[8,112,128]{2,1,0:T(8,128)S(1)} all-to-all(f32[8,112,128]{2,1,0:T(8,128)S(1)} %bitcast.9), channel_id=1, replica_groups=mesh['obj'=4,'tile'=8] {'tile'}, dimensions={0} | all-to-all | bytes 917504 | tf_op jit(solution)/shard_map/all_to_all | solution.py:528
  75.0 1.1 %shard_map.110 = (f32[576,128]{1,0:T(8,128)}, f32[72,48]{1,0:T(8,128)}) custom-call(f32[8,112,128]{2,1,0:T(8,128)S(1)} %all_to_all.11.arrived), custom_call_target="tpu_custom_call" | custom-call | tf_op jit(solution)/shard_map/pallas_call | solution.py:530
  (3 shorter events, 0.0 us)
Async XLA Ops:
  3.1 22.6 %copy-start.18 = (f32[12]{0:T(128)S(1)}, f32[12]{0:T(128)}, u32[]{:S(2)}) copy-start(f32[12]{0:T(128)} %param.17) | copy-start | bytes 148
  3.1 22.7 %copy-start.15 = (f32[12,48]{1,0:T(8,128)S(1)}, f32[12,48]{1,0:T(8,128)}, u32[]{:S(2)}) copy-start(f32[12,48]{1,0:T(8,128)} %snr_weight.1) | copy-start | bytes 6916
  3.1 22.6 %copy-start.16 = (f32[12,47]{1,0:T(8,128)S(1)}, f32[12,47]{1,0:T(8,128)}, u32[]{:S(2)}) copy-start(f32[12,47]{1,0:T(8,128)} %diffusion.1) | copy-start | bytes 6772
  3.2 22.6 %copy-start.17 = (f32[12,12]{1,0:T(8,128)S(1)}, f32[12,12]{1,0:T(8,128)}, u32[]{:S(2)}) copy-start(f32[12,12]{1,0:T(8,128)} %coupling.1) | copy-start | bytes 1732
  24.1 5.6 %collective-permute-start = (bf16[8,88,128]{2,1,0:T(8,128)(2,1)S(1)}, bf16[8,88,128]{2,1,0:T(8,128)(2,1)S(1)}, u32[]{:S(2)}, u32[]{:S(2)}) collective-permute-start(bf16[8,88,128]{2,1,0:T(8,128)(2,1)S(1)} %slice.9.refs_0_), channel_id=1, source_target_pairs={{0,16},{8,24},{16,0},{24,8},{1,17},{9,25},{17,1},{25,9},{2,18},{10... | collective-permute-start | bytes 540680 | tf_op jit(solution)/shard_map/ppermute | solution.py:385
  26.3 3.4 %copy-start.10 = (f32[3,8,128]{2,1,0:T(8,128)}, f32[3,8,128]{2,1,0:T(8,128)S(1)}, u32[]{:S(2)}) copy-start(f32[3,8,128]{2,1,0:T(8,128)S(1)} %get-tuple-element.13.refs_2_.refs_8_) | copy-start | bytes 36868
  26.3 7.4 %copy-start.5 = (f32[36,8,128]{2,1,0:T(8,128)}, f32[36,8,128]{2,1,0:T(8,128)S(1)}, u32[]{:S(2)}) copy-start(f32[36,8,128]{2,1,0:T(8,128)S(1)} %get-tuple-element.17.refs_7_) | copy-start | bytes 442372
  29.7 0.7 copy-start.3
  30.4 13.1 %collective-permute-start.2 = (bf16[8,144,128]{2,1,0:T(8,128)(2,1)}, bf16[8,144,128]{2,1,0:T(8,128)(2,1)}, u32[]{:S(2)}, u32[]{:S(2)}) collective-permute-start(bf16[8,144,128]{2,1,0:T(8,128)(2,1)} %shard_map.106.refs_0_), channel_id=1, source_target_pairs={{0,16},{8,24},{16,0},{24,8},{1,17},{9,25},{17,1},{25,9},{2,18},{10... | collective-permute-start | bytes 884744 | tf_op jit(solution)/shard_map/ppermute | solution.py:385
  31.9 1.6 %collective-permute-start.3 = (bf16[8,88,128]{2,1,0:T(8,128)(2,1)S(1)}, bf16[8,88,128]{2,1,0:T(8,128)(2,1)S(1)}, u32[]{:S(2)}, u32[]{:S(2)}) collective-permute-start(bf16[8,88,128]{2,1,0:T(8,128)(2,1)S(1)} %slice.9.refs_0_), channel_id=1, source_target_pairs={{0,8},{8,0},{16,24},{24,16},{1,9},{9,1},{17,25},{25,17},{2,10},{10... | collective-permute-start | bytes 540680 | tf_op jit(solution)/shard_map/ppermute | solution.py:385
  31.9 1.9 %collective-permute-start.4 = (bf16[8,88,128]{2,1,0:T(8,128)(2,1)}, bf16[8,88,128]{2,1,0:T(8,128)(2,1)S(1)}, u32[]{:S(2)}, u32[]{:S(2)}) collective-permute-start(bf16[8,88,128]{2,1,0:T(8,128)(2,1)} %copy-done.3), channel_id=1, source_target_pairs={{0,8},{8,0},{16,24},{24,16},{1,9},{9,1},{17,25},{25,17},{2,10},{10... | collective-permute-start | bytes 540680 | tf_op jit(solution)/shard_map/ppermute | solution.py:385
  33.0 10.7 %collective-permute-start.1 = (bf16[8,144,128]{2,1,0:T(8,128)(2,1)}, bf16[8,144,128]{2,1,0:T(8,128)(2,1)}, u32[]{:S(2)}, u32[]{:S(2)}) collective-permute-start(bf16[8,144,128]{2,1,0:T(8,128)(2,1)} %shard_map.106.refs_0_), channel_id=1, source_target_pairs={{0,8},{8,0},{16,24},{24,16},{1,9},{9,1},{17,25},{25,17},{2,10},{10... | collective-permute-start | bytes 884744 | tf_op jit(solution)/shard_map/ppermute | solution.py:385
  33.7 0.9 %copy-start.4 = (bf16[8,88,128]{2,1,0:T(8,128)(2,1)S(1)}, bf16[8,88,128]{2,1,0:T(8,128)(2,1)}, u32[]{:S(2)}) copy-start(bf16[8,88,128]{2,1,0:T(8,128)(2,1)} %copy-done.3) | copy-start | bytes 540676
  34.7 0.9 %copy-start.6 = (f32[36,8,128]{2,1,0:T(8,128)S(1)}, f32[36,8,128]{2,1,0:T(8,128)}, u32[]{:S(2)}) copy-start(f32[36,8,128]{2,1,0:T(8,128)} %copy-done.5) | copy-start | bytes 442372
  35.6 0.7 copy-start.11
  36.3 9.0 %copy-start = (bf16[8,144,128]{2,1,0:T(8,128)(2,1)S(1)}, bf16[8,144,128]{2,1,0:T(8,128)(2,1)}, u32[]{:S(2)}) copy-start(bf16[8,144,128]{2,1,0:T(8,128)(2,1)} %shard_map.106.refs_0_) | copy-start | bytes 884740
  36.3 9.0 %copy-start.12 = (f32[3,8,128]{2,1,0:T(8,128)S(1)}, f32[3,8,128]{2,1,0:T(8,128)}, u32[]{:S(2)}) copy-start(f32[3,8,128]{2,1,0:T(8,128)} %copy-done.10) | copy-start | bytes 36868
  41.3 0.9 %copy-start.1 = (f32[48,4,8,128]{3,2,1,0:T(8,128)}, f32[48,4,8,128]{3,2,1,0:T(8,128)S(1)}, u32[]{:S(2)}) copy-start(f32[48,4,8,128]{3,2,1,0:T(8,128)S(1)} %get-tuple-element.20.refs_10_) | copy-start | bytes 2359300
  42.2 0.7 copy-start.8
  42.8 0.6 copy-start.13
  43.4 1.8 %collective-permute-start.5 = (bf16[8,144,128]{2,1,0:T(8,128)(2,1)}, bf16[8,144,128]{2,1,0:T(8,128)(2,1)S(1)}, u32[]{:S(2)}, u32[]{:S(2)}) collective-permute-start(bf16[8,144,128]{2,1,0:T(8,128)(2,1)} %shard_map.108.refs_2_), channel_id=1, source_target_pairs={{0,8},{8,0},{16,24},{24,16},{1,9},{9,1},{17,25},{25,17},{2,10},{10... | collective-permute-start | bytes 884744 | tf_op jit(solution)/shard_map/ppermute | solution.py:385
  45.2 1.1 %copy-start.2 = (f32[48,4,8,128]{3,2,1,0:T(8,128)S(1)}, f32[48,4,8,128]{3,2,1,0:T(8,128)}, u32[]{:S(2)}) copy-start(f32[48,4,8,128]{3,2,1,0:T(8,128)} %copy-done.1) | copy-start | bytes 2359300
  46.4 0.9 %copy-start.7 = (f32[36,8,128]{2,1,0:T(8,128)S(1)}, f32[36,8,128]{2,1,0:T(8,128)}, u32[]{:S(2)}) copy-start(f32[36,8,128]{2,1,0:T(8,128)} %copy-done.5) | copy-start | bytes 442372
  47.3 0.9 %copy-start.9 = (f32[288,128]{1,0:T(8,128)S(1)}, f32[288,128]{1,0:T(8,128)}, u32[]{:S(2)}) copy-start(f32[288,128]{1,0:T(8,128)} %copy-done.8) | copy-start | bytes 442372
  48.2 0.7 copy-start.14

commit v4 on v3

--- a/solution.py
+++ b/solution.py
@@ -389,13 +389,14 @@
     def nothing(*refs):
         pass
 
-    anywhere = pl.BlockSpec(memory_space=pl.ANY)
+    near = pl.BlockSpec(memory_space=pltpu.VMEM)
     return pl.pallas_call(
         nothing,
         out_shape=jax.ShapeDtypeStruct(value.shape, value.dtype),
-        in_specs=[anywhere] * (1 + len(after)),
-        out_specs=anywhere,
+        in_specs=[near] * (1 + len(after)),
+        out_specs=near,
         input_output_aliases={0: 0},
+        compiler_params=pltpu.CompilerParams(vmem_limit_bytes=2**20),
     )(value, *after)
 
 
@@ -445,7 +446,7 @@
     rows = (up(spots["cells"] + 1, 8), up((steps - count) * groups * part, 8))
     short = levels // (tiles // quads)
     out_rows = up(groups * short + steps // 2 * fields, 8)
-    limit = pltpu.CompilerParams(vmem_limit_bytes=48 * 2**20)
+    limit = pltpu.CompilerParams(vmem_limit_bytes=24 * 2**20)
     in_vmem = pl.BlockSpec(memory_space=pltpu.VMEM)
     in_smem = pl.BlockSpec(memory_space=pltpu.SMEM)
     f32 = jnp.float32

time: 76.6 us -> 66 us (0.86)
  local copies, waits for them, and re-layouts: 9.88 us -> 0.15 us
  Pallas kernels: 17.7 us -> 16.7 us
    unnamed x38 -> x8, local copies, waits for them, and re-layouts: 9.02 us -> 0.03 us
    pallas_call x1, Pallas kernels: 8.64 us -> 7.67 us  [per_device(): pl.pallas_call(functools.partial(late_kernel, dims, rows[1], steps - coun...]
  transfers between devices with their start and end apart: 6 -> 6, of which waited for: 4 -> 4; matrix products, arithmetic and copies ran while one was open for 1% -> 0% of each run, Pallas kernels for 7% -> 8%
where the time goes in v4:
time: 66 us; the launch traced here: 65.7 us
  blocking collectives  38.4 us (58%)
  Pallas kernels  16.7 us (25%)
  waiting for transfers between devices  5.09 us (8%)
  starting transfers between devices  3.95 us (6%)
  between operations  1.38 us (2%)
    all_to_all x1, blocking collectives, per_device(): strips = lax.all_to_all(packed, 'tile', 0, 0, tiled=True)  20.9 us
    all_to_all x1, blocking collectives, per_device(): lax.all_to_all(result.reshape(tiles, out_rows, lanes), 'tile', 0, 0, tile...  17.5 us
    pallas_call x1, Pallas kernels, per_device(): pl.pallas_call(functools.partial(late_kernel, dims, rows[1], steps - coun...  7.67 us
    ppermute x6, waiting for transfers between devices, across(): lax.ppermute(value, 'obj', [(place, place ^ bit) for place in range(count)])  5.09 us
    pallas_call x1, Pallas kernels, per_device(): pl.pallas_call(functools.partial(early_kernel, dims, rows[0], spots, coun...  4.97 us
    ppermute x6, starting transfers between devices, across(): lax.ppermute(value, 'obj', [(place, place ^ bit) for place in range(count)])  3.95 us
    pallas_call x1, Pallas kernels, per_device(): pl.pallas_call(functools.partial(pack_kernel, dims, rows, spots), out_sha...  2.47 us
  transfers between devices with their start and end apart: 6, of which 4 were waited for; matrix products, arithmetic and copies ran while one was open for 0% of the time, Pallas kernels for 8%

profile of v4, /device:TPU:0, one launch (start us, length us, event | category | flops | bytes accessed | tf_op | source)
XLA Modules:
  0.0 65.7 jit_solution(7388553762719408774)
XLA Ops:
  0.6 2.5 %shard_map.104 = bf16[8,232,128]{2,1,0:T(8,128)(2,1)} custom-call(bf16[6,12,12,128]{3,2,1,0:T(8,128)(2,1)} %bitcast.10, f32[2,48,128]{2,1,0:T(8,128)} %bitcast.11, f32[1,128]{1,0:T(1,128)} %refs_2_.1, s32[1,128]{1,0:T(1,128)} %bitcast.12), custom_call_target="tpu_custom_call" | custom-call | bytes 3000000 | tf_op jit(solution)/shard_map/pallas_call | solution.py:456
  3.1 0.0 copy-start.3
  3.1 0.0 copy-start
  3.1 0.0 copy-start.1
  3.1 0.0 copy-start.2
  3.2 20.9 %all_to_all.10 = bf16[8,232,128]{2,1,0:T(8,128)(2,1)S(1)} all-to-all(bf16[8,232,128]{2,1,0:T(8,128)(2,1)} %shard_map.104), channel_id=1, replica_groups=mesh['obj'=4,'tile'=8] {'tile'}, dimensions={0} | all-to-all | bytes 950272 | tf_op jit(solution)/shard_map/all_to_all | solution.py:493
  24.1 1.6 %collective-permute-start = (bf16[8,88,128]{2,1,0:T(8,128)(2,1)S(1)}, bf16[8,88,128]{2,1,0:T(8,128)(2,1)S(1)}, u32[]{:S(2)}, u32[]{:S(2)}) collective-permute-start(bf16[8,88,128]{2,1,0:T(8,128)(2,1)S(1)} %slice.9.refs_0_), channel_id=1, source_target_pairs={{0,16},{8,24},{16,0},{24,8},{1,17},{9,25},{17,1},{25,9},{2,18},{10... | collective-permute-start | bytes 540680 | tf_op jit(solution)/shard_map/ppermute | solution.py:385
  25.7 0.0 copy-done.3
  25.7 0.1 copy.16.recombination
  25.8 0.0 copy-done
  25.8 0.0 copy-done.1
  25.8 0.0 copy-done.2
  25.8 0.5 shard_map.105
  26.4 3.3 %collective-permute-done.refs_1_.refs_2_ = bf16[8,88,128]{2,1,0:T(8,128)(2,1)S(1)} collective-permute-done((bf16[8,88,128]{2,1,0:T(8,128)(2,1)S(1)}, bf16[8,88,128]{2,1,0:T(8,128)(2,1)S(1)}, u32[]{:S(2)}, u32[]{:S(2)}) %collective-permute-start) | collective-permute-done | bytes 180256 | tf_op jit(solution)/shard_map/ppermute | solution.py:385
  29.7 1.5 %collective-permute-start.2 = (bf16[8,144,128]{2,1,0:T(8,128)(2,1)S(1)}, bf16[8,144,128]{2,1,0:T(8,128)(2,1)S(1)}, u32[]{:S(2)}, u32[]{:S(2)}) collective-permute-start(bf16[8,144,128]{2,1,0:T(8,128)(2,1)S(1)} %shard_map.106.refs_0_), channel_id=1, source_target_pairs={{0,16},{8,24},{16,0},{24,8},{1,17},{9,25},{17,1},{25,9},{2,18},{10... | collective-permute-start | bytes 884744 | tf_op jit(solution)/shard_map/ppermute | solution.py:385
  31.2 0.0 collective-permute-start.3
  31.2 0.5 collective-permute-start.4
  32.3 0.1 collective-permute-start.1
  32.4 0.2 collective-permute-done.3.refs_1_
  32.6 0.3 collective-permute-done.4.refs_3_
  32.8 5.0 %shard_map.107 = (f32[144,16,128]{2,1,0:T(8,128)S(1)}, f32[48,4,8,128]{3,2,1,0:T(8,128)S(1)}, f32[288,128]{1,0:T(8,128)S(1)}, f32[2,8,128]{2,1,0:T(8,128)S(1)}) custom-call(s32[1]{0:T(128)S(6)} %copy.21.measure_step, bf16[8,88,128]{2,1,0:T(8,128)(2,1)S(1)} %slice.9.refs_0_, bf16[8,88,128]{2,1,0:T(8,128)(2,1)S(1)} %collective-permute-done.3.refs_1_, ...), custom_call_target="tpu_custom_call" | custom-call | bytes 15000000 | tf_op jit(solution)/shard_map/pallas_call | solution.py:499
  37.8 0.0 collective-permute-done.2.refs_0_
  37.8 0.3 collective-permute-start.5
  38.2 0.0 collective-permute-done.1.refs_1_
  38.2 1.3 %collective-permute-done.5.refs_3_ = bf16[8,144,128]{2,1,0:T(8,128)(2,1)S(1)} collective-permute-done((bf16[8,144,128]{2,1,0:T(8,128)(2,1)S(1)}, bf16[8,144,128]{2,1,0:T(8,128)(2,1)S(1)}, u32[]{:S(2)}, u32[]{:S(2)}) %collective-permute-start.5) | collective-permute-done | bytes 294944 | tf_op jit(solution)/shard_map/ppermute | solution.py:385
  39.5 7.7 %shard_map.109 = f32[896,128]{1,0:T(8,128)S(1)} custom-call(s32[1]{0:T(128)S(6)} %copy.21.measure_step, bf16[8,144,128]{2,1,0:T(8,128)(2,1)S(1)} %shard_map.106.refs_0_, bf16[8,144,128]{2,1,0:T(8,128)(2,1)S(1)} %collective-permute-done.1.refs_1_, bf16[8,144,128]{2,1,0:T(8,128)(2,1)S(1)} %shard_map.108.refs_2_, ...), custom_call_target="tpu_custom_call" | custom-call | bytes 15000000 | tf_op jit(solution)/shard_map/pallas_call | solution.py:515
  47.2 17.5 %all_to_all.11.arrived = f32[8,112,128]{2,1,0:T(8,128)S(1)} all-to-all(f32[8,112,128]{2,1,0:T(8,128)S(1)} %bitcast.9), channel_id=1, replica_groups=mesh['obj'=4,'tile'=8] {'tile'}, dimensions={0} | all-to-all | bytes 917504 | tf_op jit(solution)/shard_map/all_to_all | solution.py:529
  64.6 1.1 %shard_map.110 = (f32[576,128]{1,0:T(8,128)}, f32[72,48]{1,0:T(8,128)}) custom-call(f32[8,112,128]{2,1,0:T(8,128)S(1)} %all_to_all.11.arrived), custom_call_target="tpu_custom_call" | custom-call | tf_op jit(solution)/shard_map/pallas_call | solution.py:531
  (4 shorter events, 0.0 us)
Async XLA Ops:
  3.1 22.6 %copy-start.3 = (f32[12]{0:T(128)S(1)}, f32[12]{0:T(128)}, u32[]{:S(2)}) copy-start(f32[12]{0:T(128)} %param.17) | copy-start | bytes 148
  3.1 22.7 %copy-start = (f32[12,48]{1,0:T(8,128)S(1)}, f32[12,48]{1,0:T(8,128)}, u32[]{:S(2)}) copy-start(f32[12,48]{1,0:T(8,128)} %snr_weight.1) | copy-start | bytes 6916
  3.1 22.6 %copy-start.1 = (f32[12,47]{1,0:T(8,128)S(1)}, f32[12,47]{1,0:T(8,128)}, u32[]{:S(2)}) copy-start(f32[12,47]{1,0:T(8,128)} %diffusion.1) | copy-start | bytes 6772
  3.1 22.6 %copy-start.2 = (f32[12,12]{1,0:T(8,128)S(1)}, f32[12,12]{1,0:T(8,128)}, u32[]{:S(2)}) copy-start(f32[12,12]{1,0:T(8,128)} %coupling.1) | copy-start | bytes 1732
  24.1 5.6 %collective-permute-start = (bf16[8,88,128]{2,1,0:T(8,128)(2,1)S(1)}, bf16[8,88,128]{2,1,0:T(8,128)(2,1)S(1)}, u32[]{:S(2)}, u32[]{:S(2)}) collective-permute-start(bf16[8,88,128]{2,1,0:T(8,128)(2,1)S(1)} %slice.9.refs_0_), channel_id=1, source_target_pairs={{0,16},{8,24},{16,0},{24,8},{1,17},{9,25},{17,1},{25,9},{2,18},{10... | collective-permute-start | bytes 540680 | tf_op jit(solution)/shard_map/ppermute | solution.py:385
  29.7 8.1 %collective-permute-start.2 = (bf16[8,144,128]{2,1,0:T(8,128)(2,1)S(1)}, bf16[8,144,128]{2,1,0:T(8,128)(2,1)S(1)}, u32[]{:S(2)}, u32[]{:S(2)}) collective-permute-start(bf16[8,144,128]{2,1,0:T(8,128)(2,1)S(1)} %shard_map.106.refs_0_), channel_id=1, source_target_pairs={{0,16},{8,24},{16,0},{24,8},{1,17},{9,25},{17,1},{25,9},{2,18},{10... | collective-permute-start | bytes 884744 | tf_op jit(solution)/shard_map/ppermute | solution.py:385
  31.2 1.4 %collective-permute-start.3 = (bf16[8,88,128]{2,1,0:T(8,128)(2,1)S(1)}, bf16[8,88,128]{2,1,0:T(8,128)(2,1)S(1)}, u32[]{:S(2)}, u32[]{:S(2)}) collective-permute-start(bf16[8,88,128]{2,1,0:T(8,128)(2,1)S(1)} %slice.9.refs_0_), channel_id=1, source_target_pairs={{0,8},{8,0},{16,24},{24,16},{1,9},{9,1},{17,25},{25,17},{2,10},{10... | collective-permute-start | bytes 540680 | tf_op jit(solution)/shard_map/ppermute | solution.py:385
  31.2 1.7 %collective-permute-start.4 = (bf16[8,88,128]{2,1,0:T(8,128)(2,1)S(1)}, bf16[8,88,128]{2,1,0:T(8,128)(2,1)S(1)}, u32[]{:S(2)}, u32[]{:S(2)}) collective-permute-start(bf16[8,88,128]{2,1,0:T(8,128)(2,1)S(1)} %collective-permute-done.refs_1_.refs_2_), channel_id=1, source_target_pairs={{0,8},{8,0},{16,24},{24,16},{1,9},{9,1},{17,25},{25,17},{2,10},{10... | collective-permute-start | bytes 540680 | tf_op jit(solution)/shard_map/ppermute | solution.py:385
  32.3 5.8 %collective-permute-start.1 = (bf16[8,144,128]{2,1,0:T(8,128)(2,1)S(1)}, bf16[8,144,128]{2,1,0:T(8,128)(2,1)S(1)}, u32[]{:S(2)}, u32[]{:S(2)}) collective-permute-start(bf16[8,144,128]{2,1,0:T(8,128)(2,1)S(1)} %shard_map.106.refs_0_), channel_id=1, source_target_pairs={{0,8},{8,0},{16,24},{24,16},{1,9},{9,1},{17,25},{25,17},{2,10},{10... | collective-permute-start | bytes 884744 | tf_op jit(solution)/shard_map/ppermute | solution.py:385
  37.8 1.6 %collective-permute-start.5 = (bf16[8,144,128]{2,1,0:T(8,128)(2,1)S(1)}, bf16[8,144,128]{2,1,0:T(8,128)(2,1)S(1)}, u32[]{:S(2)}, u32[]{:S(2)}) collective-permute-start(bf16[8,144,128]{2,1,0:T(8,128)(2,1)S(1)} %shard_map.108.refs_2_), channel_id=1, source_target_pairs={{0,8},{8,0},{16,24},{24,16},{1,9},{9,1},{17,25},{25,17},{2,10},{10... | collective-permute-start | bytes 884744 | tf_op jit(solution)/shard_map/ppermute | solution.py:385

commit v5 on v4

--- a/solution.py
+++ b/solution.py
@@ -1,4 +1,5 @@
 import functools
+import math
 
 import jax
 import jax.numpy as jnp
@@ -13,6 +14,9 @@
 window = lanes // quads
 exact = lax.Precision.HIGHEST
 early_steps = 2
+most = 32760.0
+finest = 2.0**30
+octave = 0.25 * math.log(2.0)
 
 
 def up(value, unit):
@@ -280,7 +284,7 @@
 def late_kernel(dims, rows, count, parts, out_rows, measure_step, *refs):
     pieces, refs = refs[:parts], refs[parts:]
     tables, refs = refs[:5], refs[5:]
-    given, coefs, early_sums, cells, out, wide, adjoint, sums, solving, lit = refs
+    given, coefs, early_sums, cells, out, wide, adjoint, sums, solving, lit, sent = refs
     steps, groups, part, tiles, own, halo = dims
     levels = adjoint.shape[0] // groups
     fields = groups * quads
@@ -307,6 +311,7 @@
     stack = tiles // quads
     short = levels // stack
     home = (lane_iota(cell) % window) // own
+    largest = jnp.zeros(cell, jnp.float32)
     for group in range(groups):
         for level in range(short):
             whole = jnp.zeros(cell, jnp.float32)
@@ -314,35 +319,57 @@
                 value = adjoint[(high * short + level) * groups + group, 0:tiles]
                 turned = pltpu.roll(value, (high * own - halo) % lanes, 1)
                 whole = jnp.where(home == high, turned, whole)
-            out[pl.ds(group * short + level, tiles, stride=out_rows), :] = whole
+            largest = jnp.maximum(largest, jnp.abs(whole))
+            sent[pl.ds(group * short + level, tiles, stride=out_rows), :] = whole
+    power = exponent(largest)
+    factor = jnp.exp(-octave * power) * most
+    base = groups * short
+
     shape = (8, lanes)
     chosen = jnp.where(lax.broadcasted_iota(jnp.int32, shape, 0) == lane_iota(shape) // window, 1.0, 0.0)
-    base = groups * short
-    gap = jnp.zeros((quads, lanes // 2 - levels), jnp.float32)
-    half = steps // 2
-
-    def summed(back, group):
-        early = steps - count
+    early = steps - count
+    lines = []
+    for back in range(steps):
         table, place = (early_sums, back) if back < early else (sums, back - early)
-        return lax.dot_general(
-            chosen,
-            table[pl.ds(place * levels * groups + group, levels, stride=groups), :],
-            (((1,), (1,)), ((), ())),
-            precision=exact,
-            preferred_element_type=jnp.float32,
-        )[:quads]
-
-    for back in range(half):
         for group in range(groups):
-            line = jnp.concatenate([summed(back, group), gap, summed(back + half, group), gap], axis=1)
-            for longitude in range(tiles):
-                at = longitude * out_rows + base + back * fields + group * quads
-                out[at : at + quads, :] = line
+            lines.append(table[pl.ds(place * levels * groups + group, levels, stride=groups), :])
+    width = up(steps * groups * levels, lanes)
+    slack = width - steps * groups * levels
+    total = lax.dot_general(
+        chosen,
+        jnp.concatenate(lines + [jnp.zeros((slack, lanes), jnp.float32)], axis=0),
+        (((1,), (1,)), ((), ())),
+        precision=exact,
+        preferred_element_type=jnp.float32,
+    )
+    peak = exponent(jnp.max(jnp.abs(total), axis=(0, 1), keepdims=True))
+    fixed = jnp.round(total * (jnp.exp(-octave * peak) * finest))
+    coarse = jnp.floor(fixed * (1.0 / 65536.0) + 0.5)
+    rest = fixed - coarse * 65536.0
+    tall = width // lanes
+    free = lane_iota((quads, lanes)) >= lanes - slack
     for longitude in range(tiles):
-        at = longitude * out_rows + base + half * fields
-        if at < (longitude + 1) * out_rows:
-            rest = (longitude + 1) * out_rows - at
-            out[at : at + rest, :] = jnp.zeros((rest, lanes), jnp.float32)
+        at = longitude * out_rows
+        sent[at : at + base, :] = jnp.round(sent[at : at + base, :] * factor[longitude : longitude + 1])
+        line = power[longitude : longitude + 1]
+        shown = jnp.concatenate([pltpu.roll(line, (lanes - window * (quad + 1)) % lanes, 1) for quad in range(quads)], axis=0)
+        for tall_at in range(tall):
+            high = coarse[:quads, tall_at * lanes : (tall_at + 1) * lanes]
+            low = rest[:quads, tall_at * lanes : (tall_at + 1) * lanes]
+            if tall_at == tall - 1:
+                high = jnp.where(free, shown, high)
+                low = jnp.where(free, peak, low)
+            place = at + base + tall_at * quads
+            sent[place : place + quads, :] = high
+            sent[place + tall * quads : place + (tall + 1) * quads, :] = low
+        used = base + 2 * tall * quads
+        if used < out_rows:
+            sent[at + used : at + out_rows, :] = jnp.zeros((out_rows - used, lanes), jnp.float32)
+        out[longitude] = sent[at : at + out_rows, :].astype(jnp.int32).astype(jnp.int16)
+
+
+def exponent(largest):
+    return jnp.ceil(jnp.log(jnp.maximum(largest, 1e-30)) * (1.0 / octave) + 0.01)
 
 
 def unpack_kernel(dims, arrived, state_adjoint, driver_grad):
@@ -350,8 +377,23 @@
     stack = tiles // quads
     short = levels // stack
     base = groups * short
-    half = steps // 2
-    values = [arrived[tile, 0:base, :] for tile in range(tiles)]
+    width = up(steps * groups * levels, lanes)
+    slack = width - steps * groups * levels
+    tall = width // lanes
+    quarter = lane_iota((1, lanes)) // window
+    values = []
+    total = jnp.zeros((tall * quads, lanes), jnp.float32)
+    for tile in range(tiles):
+        whole = arrived[tile].astype(jnp.int32).astype(jnp.float32)
+        coarse = whole[base : base + tall * quads]
+        rest = whole[base + tall * quads : base + 2 * tall * quads]
+        power = jnp.zeros((1, lanes), jnp.float32)
+        for quad in range(quads):
+            line = coarse[(tall - 1) * quads + quad : (tall - 1) * quads + quad + 1]
+            power = jnp.where(quarter == quad, pltpu.roll(line, window * (quad + 1) % lanes, 1), power)
+        values.append(whole[0:base] * (jnp.exp(octave * power) * (1.0 / most)))
+        peak = rest[(tall - 1) * quads : (tall - 1) * quads + 1, lanes - 1 : lanes]
+        total = total + (coarse * 65536.0 + rest) * (jnp.exp(octave * peak) * (1.0 / finest))
     home = lane_iota((base, lanes)) // own
     apart = 1
     while apart < tiles:
@@ -368,16 +410,13 @@
             for group in range(groups):
                 at = (group * quads + quad) * levels + high * short
                 state_adjoint[at : at + short, :] = values[quad * stack + high][group * short : (group + 1) * short]
-    total = arrived[0, base : base + half * fields, :]
-    for tile in range(1, tiles):
-        total = total + arrived[tile, base : base + half * fields, :]
     total = total / cells
-    late = pltpu.roll(total, lanes // 2, 1)
-    for back in range(half):
-        at = (steps - 1 - back) * fields
-        driver_grad[at : at + fields, :] = total[back * fields : (back + 1) * fields, :levels]
-        at = (half - 1 - back) * fields
-        driver_grad[at : at + fields, :] = late[back * fields : (back + 1) * fields, :levels]
+    total = jnp.concatenate([total[at * quads : (at + 1) * quads] for at in range(tall)], axis=1)
+    for back in range(steps):
+        for group in range(groups):
+            at = (steps - 1 - back) * fields + group * quads
+            start = (back * groups + group) * levels
+            driver_grad[at : at + quads, :] = total[:, start : start + levels]
 
 
 def across(value, bit):
@@ -386,17 +425,16 @@
 
 
 def hold(value, *after):
-    def nothing(*refs):
-        pass
+    def copy(source, *refs):
+        refs[-1][...] = source[...]
 
     near = pl.BlockSpec(memory_space=pltpu.VMEM)
     return pl.pallas_call(
-        nothing,
+        copy,
         out_shape=jax.ShapeDtypeStruct(value.shape, value.dtype),
-        in_specs=[near] * (1 + len(after)),
+        in_specs=[near] + [pl.BlockSpec(memory_space=pl.ANY)] * len(after),
         out_specs=near,
-        input_output_aliases={0: 0},
-        compiler_params=pltpu.CompilerParams(vmem_limit_bytes=2**20),
+        compiler_params=pltpu.CompilerParams(vmem_limit_bytes=2 * 2**20),
     )(value, *after)
 
 
@@ -445,7 +483,7 @@
     spots["cells"] = spots["wind"] + part
     rows = (up(spots["cells"] + 1, 8), up((steps - count) * groups * part, 8))
     short = levels // (tiles // quads)
-    out_rows = up(groups * short + steps // 2 * fields, 8)
+    out_rows = up(groups * short + 2 * quads * up(steps * groups * levels, lanes) // lanes, 16)
     limit = pltpu.CompilerParams(vmem_limit_bytes=24 * 2**20)
     in_vmem = pl.BlockSpec(memory_space=pltpu.VMEM)
     in_smem = pl.BlockSpec(memory_space=pltpu.SMEM)
@@ -514,7 +552,7 @@
     late = over_cores({apart: hold(late[apart], known[3]) if apart else late[apart] for apart in late})
     result = pl.pallas_call(
         functools.partial(late_kernel, dims, rows[1], steps - count, parts, out_rows),
-        out_shape=jax.ShapeDtypeStruct((tiles * out_rows, lanes), f32),
+        out_shape=jax.ShapeDtypeStruct((tiles, out_rows, lanes), jnp.int16),
         in_specs=[in_smem] + [in_vmem] * (parts + 9),
         out_specs=in_vmem,
         scratch_shapes=[
@@ -522,11 +560,12 @@
             pltpu.VMEM((levels * groups, 2 * tiles, lanes), f32),
             pltpu.VMEM(((steps - count) * groups * levels, lanes), f32),
         ]
-        + work,
+        + work
+        + [pltpu.VMEM((tiles * out_rows, lanes), f32)],
         compiler_params=limit,
         cost_estimate=cost(5),
     )(measure_step, *late, *tables, *known)
-    home = lax.all_to_all(result.reshape(tiles, out_rows, lanes), "tile", 0, 0, tiled=True)
+    home = lax.all_to_all(result, "tile", 0, 0, tiled=True)
 
     state_adjoint, driver_grad = pl.pallas_call(
         functools.partial(unpack_kernel, (steps, groups, levels, fields, tiles, own, tiles * lanes)),

time: 66 us -> 61.8 us (0.936)
  blocking collectives: 38.4 us -> 34.1 us
    all_to_all x1, blocking collectives: 17.5 us -> 13.2 us  [per_device(): home = lax.all_to_all(result, 'tile', 0, 0, tiled=True)]
  transfers between devices with their start and end apart: 6 -> 6, of which waited for: 4 -> 4; matrix products, arithmetic and copies ran while one was open for 0% -> 0% of each run, Pallas kernels for 8% -> 9%
where the time goes in v5:
time: 61.8 us; the launch traced here: 61.5 us
  blocking collectives  34.1 us (55%)
  Pallas kernels  16.7 us (27%)
  waiting for transfers between devices  5.09 us (8%)
  starting transfers between devices  4.02 us (7%)
  between operations  1.39 us (2%)
    all_to_all x1, blocking collectives, per_device(): strips = lax.all_to_all(packed, 'tile', 0, 0, tiled=True)  20.9 us
    all_to_all x1, blocking collectives, per_device(): home = lax.all_to_all(result, 'tile', 0, 0, tiled=True)  13.2 us
    pallas_call x1, Pallas kernels, per_device(): pl.pallas_call(functools.partial(late_kernel, dims, rows[1], steps - coun...  7.59 us
    ppermute x6, waiting for transfers between devices, across(): lax.ppermute(value, 'obj', [(place, place ^ bit) for place in range(count)])  5.09 us
    pallas_call x1, Pallas kernels, per_device(): pl.pallas_call(functools.partial(early_kernel, dims, rows[0], spots, coun...  4.95 us
    ppermute x6, starting transfers between devices, across(): lax.ppermute(value, 'obj', [(place, place ^ bit) for place in range(count)])  4.02 us
    pallas_call x1, Pallas kernels, per_device(): pl.pallas_call(functools.partial(pack_kernel, dims, rows, spots), out_sha...  2.47 us
  transfers between devices with their start and end apart: 6, of which 4 were waited for; matrix products, arithmetic and copies ran while one was open for 0% of the time, Pallas kernels for 9%

profile of v5, /device:TPU:0, one launch (start us, length us, event | category | flops | bytes accessed | tf_op | source)
XLA Modules:
  0.0 61.5 jit_solution(4460532668994625508)
XLA Ops:
  0.6 2.5 %shard_map.104 = bf16[8,232,128]{2,1,0:T(8,128)(2,1)} custom-call(bf16[6,12,12,128]{3,2,1,0:T(8,128)(2,1)} %bitcast.8, f32[2,48,128]{2,1,0:T(8,128)} %bitcast.9, f32[1,128]{1,0:T(1,128)} %refs_2_.1, s32[1,128]{1,0:T(1,128)} %bitcast.10), custom_call_target="tpu_custom_call" | custom-call | bytes 3000000 | tf_op jit(solution)/shard_map/pallas_call | solution.py:494
  3.1 0.0 copy-start.3
  3.1 0.0 copy-start
  3.1 0.0 copy-start.1
  3.1 0.0 copy-start.2
  3.2 20.9 %all_to_all.10 = bf16[8,232,128]{2,1,0:T(8,128)(2,1)S(1)} all-to-all(bf16[8,232,128]{2,1,0:T(8,128)(2,1)} %shard_map.104), channel_id=1, replica_groups=mesh['obj'=4,'tile'=8] {'tile'}, dimensions={0} | all-to-all | bytes 950272 | tf_op jit(solution)/shard_map/all_to_all | solution.py:531
  24.1 1.6 %collective-permute-start = (bf16[8,88,128]{2,1,0:T(8,128)(2,1)S(1)}, bf16[8,88,128]{2,1,0:T(8,128)(2,1)S(1)}, u32[]{:S(2)}, u32[]{:S(2)}) collective-permute-start(bf16[8,88,128]{2,1,0:T(8,128)(2,1)S(1)} %slice.9.refs_0_), channel_id=1, source_target_pairs={{0,16},{8,24},{16,0},{24,8},{1,17},{9,25},{17,1},{25,9},{2,18},{10... | collective-permute-start | bytes 540680 | tf_op jit(solution)/shard_map/ppermute | solution.py:424
  25.7 0.0 copy-done.3
  25.7 0.1 copy.14.recombination
  25.8 0.0 copy-done
  25.8 0.0 copy-done.1
  25.8 0.0 copy-done.2
  25.8 0.5 shard_map.105
  26.4 3.3 %collective-permute-done.refs_0_.refs_2_ = bf16[8,88,128]{2,1,0:T(8,128)(2,1)S(1)} collective-permute-done((bf16[8,88,128]{2,1,0:T(8,128)(2,1)S(1)}, bf16[8,88,128]{2,1,0:T(8,128)(2,1)S(1)}, u32[]{:S(2)}, u32[]{:S(2)}) %collective-permute-start) | collective-permute-done | bytes 180256 | tf_op jit(solution)/shard_map/ppermute | solution.py:424
  29.7 1.6 %collective-permute-start.2 = (bf16[8,144,128]{2,1,0:T(8,128)(2,1)S(1)}, bf16[8,144,128]{2,1,0:T(8,128)(2,1)S(1)}, u32[]{:S(2)}, u32[]{:S(2)}) collective-permute-start(bf16[8,144,128]{2,1,0:T(8,128)(2,1)S(1)} %shard_map.106.refs_0_), channel_id=1, source_target_pairs={{0,16},{8,24},{16,0},{24,8},{1,17},{9,25},{17,1},{25,9},{2,18},{10... | collective-permute-start | bytes 884744 | tf_op jit(solution)/shard_map/ppermute | solution.py:424
  31.3 0.0 collective-permute-start.3
  31.3 0.5 collective-permute-start.4
  32.4 0.1 collective-permute-start.1
  32.5 0.2 collective-permute-done.3.refs_1_
  32.7 0.3 collective-permute-done.4.refs_3_
  32.9 5.0 %shard_map.107 = (f32[144,16,128]{2,1,0:T(8,128)S(1)}, f32[48,4,8,128]{3,2,1,0:T(8,128)S(1)}, f32[288,128]{1,0:T(8,128)S(1)}, f32[2,8,128]{2,1,0:T(8,128)S(1)}) custom-call(s32[1]{0:T(128)S(6)} %copy.17.measure_step, bf16[8,88,128]{2,1,0:T(8,128)(2,1)S(1)} %slice.9.refs_0_, bf16[8,88,128]{2,1,0:T(8,128)(2,1)S(1)} %collective-permute-done.3.refs_1_, ...), custom_call_target="tpu_custom_call" | custom-call | bytes 15000000 | tf_op jit(solution)/shard_map/pallas_call | solution.py:537
  37.9 0.0 collective-permute-done.2.source
  37.9 0.3 collective-permute-start.5
  38.2 0.0 collective-permute-done.1.refs_1_
  38.3 1.3 %collective-permute-done.5.refs_3_ = bf16[8,144,128]{2,1,0:T(8,128)(2,1)S(1)} collective-permute-done((bf16[8,144,128]{2,1,0:T(8,128)(2,1)S(1)}, bf16[8,144,128]{2,1,0:T(8,128)(2,1)S(1)}, u32[]{:S(2)}, u32[]{:S(2)}) %collective-permute-start.5) | collective-permute-done | bytes 294944 | tf_op jit(solution)/shard_map/ppermute | solution.py:424
  39.6 7.6 %shard_map.109 = s16[8,128,128]{2,1,0:T(8,128)(2,1)S(1)} custom-call(s32[1]{0:T(128)S(6)} %copy.17.measure_step, bf16[8,144,128]{2,1,0:T(8,128)(2,1)S(1)} %shard_map.106.refs_0_, bf16[8,144,128]{2,1,0:T(8,128)(2,1)S(1)} %collective-permute-done.1.refs_1_, bf16[8,144,128]{2,1,0:T(8,128)(2,1)S(1)} %shard_map.108.refs_2_, ...), custom_call_target="tpu_custom_call" | custom-call | bytes 15000000 | tf_op jit(solution)/shard_map/pallas_call | solution.py:553
  47.2 13.2 %all_to_all.11.arrived = s16[8,128,128]{2,1,0:T(8,128)(2,1)S(1)} all-to-all(s16[8,128,128]{2,1,0:T(8,128)(2,1)S(1)} %shard_map.109), channel_id=1, replica_groups=mesh['obj'=4,'tile'=8] {'tile'}, dimensions={0} | all-to-all | bytes 524288 | tf_op jit(solution)/shard_map/all_to_all | solution.py:568
  60.4 1.1 %shard_map.110 = (f32[576,128]{1,0:T(8,128)}, f32[72,48]{1,0:T(8,128)}) custom-call(s16[8,128,128]{2,1,0:T(8,128)(2,1)S(1)} %all_to_all.11.arrived), custom_call_target="tpu_custom_call" | custom-call | tf_op jit(solution)/shard_map/pallas_call | solution.py:570
  (4 shorter events, 0.1 us)
Async XLA Ops:
  3.1 22.6 %copy-start.3 = (f32[12]{0:T(128)S(1)}, f32[12]{0:T(128)}, u32[]{:S(2)}) copy-start(f32[12]{0:T(128)} %param.17) | copy-start | bytes 148
  3.1 22.7 %copy-start = (f32[12,48]{1,0:T(8,128)S(1)}, f32[12,48]{1,0:T(8,128)}, u32[]{:S(2)}) copy-start(f32[12,48]{1,0:T(8,128)} %snr_weight.1) | copy-start | bytes 6916
  3.1 22.6 %copy-start.1 = (f32[12,47]{1,0:T(8,128)S(1)}, f32[12,47]{1,0:T(8,128)}, u32[]{:S(2)}) copy-start(f32[12,47]{1,0:T(8,128)} %diffusion.1) | copy-start | bytes 6772
  3.1 22.6 %copy-start.2 = (f32[12,12]{1,0:T(8,128)S(1)}, f32[12,12]{1,0:T(8,128)}, u32[]{:S(2)}) copy-start(f32[12,12]{1,0:T(8,128)} %coupling.1) | copy-start | bytes 1732
  24.1 5.6 %collective-permute-start = (bf16[8,88,128]{2,1,0:T(8,128)(2,1)S(1)}, bf16[8,88,128]{2,1,0:T(8,128)(2,1)S(1)}, u32[]{:S(2)}, u32[]{:S(2)}) collective-permute-start(bf16[8,88,128]{2,1,0:T(8,128)(2,1)S(1)} %slice.9.refs_0_), channel_id=1, source_target_pairs={{0,16},{8,24},{16,0},{24,8},{1,17},{9,25},{17,1},{25,9},{2,18},{10... | collective-permute-start | bytes 540680 | tf_op jit(solution)/shard_map/ppermute | solution.py:424
  29.7 8.2 %collective-permute-start.2 = (bf16[8,144,128]{2,1,0:T(8,128)(2,1)S(1)}, bf16[8,144,128]{2,1,0:T(8,128)(2,1)S(1)}, u32[]{:S(2)}, u32[]{:S(2)}) collective-permute-start(bf16[8,144,128]{2,1,0:T(8,128)(2,1)S(1)} %shard_map.106.refs_0_), channel_id=1, source_target_pairs={{0,16},{8,24},{16,0},{24,8},{1,17},{9,25},{17,1},{25,9},{2,18},{10... | collective-permute-start | bytes 884744 | tf_op jit(solution)/shard_map/ppermute | solution.py:424
  31.3 1.4 %collective-permute-start.3 = (bf16[8,88,128]{2,1,0:T(8,128)(2,1)S(1)}, bf16[8,88,128]{2,1,0:T(8,128)(2,1)S(1)}, u32[]{:S(2)}, u32[]{:S(2)}) collective-permute-start(bf16[8,88,128]{2,1,0:T(8,128)(2,1)S(1)} %slice.9.refs_0_), channel_id=1, source_target_pairs={{0,8},{8,0},{16,24},{24,16},{1,9},{9,1},{17,25},{25,17},{2,10},{10... | collective-permute-start | bytes 540680 | tf_op jit(solution)/shard_map/ppermute | solution.py:424
  31.3 1.7 %collective-permute-start.4 = (bf16[8,88,128]{2,1,0:T(8,128)(2,1)S(1)}, bf16[8,88,128]{2,1,0:T(8,128)(2,1)S(1)}, u32[]{:S(2)}, u32[]{:S(2)}) collective-permute-start(bf16[8,88,128]{2,1,0:T(8,128)(2,1)S(1)} %collective-permute-done.refs_0_.refs_2_), channel_id=1, source_target_pairs={{0,8},{8,0},{16,24},{24,16},{1,9},{9,1},{17,25},{25,17},{2,10},{10... | collective-permute-start | bytes 540680 | tf_op jit(solution)/shard_map/ppermute | solution.py:424
  32.4 5.8 %collective-permute-start.1 = (bf16[8,144,128]{2,1,0:T(8,128)(2,1)S(1)}, bf16[8,144,128]{2,1,0:T(8,128)(2,1)S(1)}, u32[]{:S(2)}, u32[]{:S(2)}) collective-permute-start(bf16[8,144,128]{2,1,0:T(8,128)(2,1)S(1)} %shard_map.106.refs_0_), channel_id=1, source_target_pairs={{0,8},{8,0},{16,24},{24,16},{1,9},{9,1},{17,25},{25,17},{2,10},{10... | collective-permute-start | bytes 884744 | tf_op jit(solution)/shard_map/ppermute | solution.py:424
  37.9 1.6 %collective-permute-start.5 = (bf16[8,144,128]{2,1,0:T(8,128)(2,1)S(1)}, bf16[8,144,128]{2,1,0:T(8,128)(2,1)S(1)}, u32[]{:S(2)}, u32[]{:S(2)}) collective-permute-start(bf16[8,144,128]{2,1,0:T(8,128)(2,1)S(1)} %shard_map.108.refs_2_), channel_id=1, source_target_pairs={{0,8},{8,0},{16,24},{24,16},{1,9},{9,1},{17,25},{25,17},{2,10},{10... | collective-permute-start | bytes 884744 | tf_op jit(solution)/shard_map/ppermute | solution.py:424

commit v6 on v5

--- a/solution.py
+++ b/solution.py
@@ -13,7 +13,7 @@
 quads = 4
 window = lanes // quads
 exact = lax.Precision.HIGHEST
-early_steps = 2
+early_steps = 3
 most = 32760.0
 finest = 2.0**30
 octave = 0.25 * math.log(2.0)
@@ -28,7 +28,7 @@
 
 
 def pack_kernel(dims, rows, spots, *refs):
-    outside, out, staged, inside, arrival = refs[:4], refs[4], refs[5], refs[6:10], refs[10]
+    outside, first, second, staged, inside, arrival = refs[:4], refs[4], refs[5], refs[6], refs[7:11], refs[11]
     copies = [pltpu.make_async_copy(outside[i], inside[i], arrival.at[i]) for i in range(4)]
     for copy in copies:
         copy.start()
@@ -72,7 +72,9 @@
         inside = own * tile - halo + lane % window
         pick = (row == wanted) & (inside >= 0) & (inside < lanes)
         pick = jnp.where(pick, 1.0, 0.0).astype(jnp.bfloat16)
-        out[tile] = jnp.dot(source, pick, preferred_element_type=jnp.float32).astype(jnp.bfloat16)
+        cut = jnp.dot(source, pick, preferred_element_type=jnp.float32).astype(jnp.bfloat16)
+        first[tile] = cut[: rows[0]]
+        second[tile] = cut[rows[0] :]
 
 
 def spread(values, group):
@@ -162,14 +164,13 @@
     latitude = own * lax.axis_index("tile") - halo + lane_iota(cell) % window
     inside = jnp.where((latitude >= 0) & (latitude < lanes), 1.0, 0.0)
     centre = (1.0 - 4.0 * smoothing) * inside
-    block = 12 if levels % 12 == 0 else levels
+    block = levels
     together = 3 if block % 3 == 0 else 1
     nothing = tuple(jnp.zeros(cell, jnp.float32) for _ in range(groups))
 
     def step(back, carry):
         moment = first - back
-        upcoming = jnp.where((measure_step[0] == moment) & (moment > 0), 1.0, 0.0)
-        scored = upcoming * mask
+        scored = jnp.where((measure_step[...] == moment) & (moment > 0), 1.0, 0.0) * mask
 
         def forward(at, before):
             before = list(before)
@@ -271,7 +272,7 @@
         coefs[level, 2] = pltpu.roll(smoothing + 0.5 * north, lanes - 1, 1) * inside
         coefs[level, 3] = pltpu.roll(smoothing - 0.5 * north, 1, 1) * inside
 
-    scored = jnp.where(measure_step[0] == steps, 1.0, 0.0) * mask
+    scored = jnp.where(measure_step[...] == steps, 1.0, 0.0) * mask
     for row in range(levels * groups):
         begin = scored * tables[0][row]
         adjoint[row, 0:tiles] = begin
@@ -481,21 +482,20 @@
     dims = (steps, groups, part, tiles, own, halo)
     spots = {"wind": count * groups * part}
     spots["cells"] = spots["wind"] + part
-    rows = (up(spots["cells"] + 1, 8), up((steps - count) * groups * part, 8))
+    rows = (up(spots["cells"] + 1, 16), up((steps - count) * groups * part, 16))
     short = levels // (tiles // quads)
     out_rows = up(groups * short + 2 * quads * up(steps * groups * levels, lanes) // lanes, 16)
     limit = pltpu.CompilerParams(vmem_limit_bytes=24 * 2**20)
     in_vmem = pl.BlockSpec(memory_space=pltpu.VMEM)
-    in_smem = pl.BlockSpec(memory_space=pltpu.SMEM)
     f32 = jnp.float32
     cell = (tiles, lanes)
     full = (levels * groups,) + cell
 
-    packed = pl.pallas_call(
+    packed, packed_late = pl.pallas_call(
         functools.partial(pack_kernel, dims, rows, spots),
-        out_shape=jax.ShapeDtypeStruct((tiles, sum(rows), lanes), jnp.bfloat16),
+        out_shape=tuple(jax.ShapeDtypeStruct((tiles, size, lanes), jnp.bfloat16) for size in rows),
         in_specs=[pl.BlockSpec(memory_space=pltpu.HBM)] * 4,
-        out_specs=in_vmem,
+        out_specs=(in_vmem, in_vmem),
         scratch_shapes=[
             pltpu.VMEM((quads, sum(rows), lanes), f32),
             pltpu.VMEM((steps, fields, part, lanes), checkpoints.dtype),
@@ -529,9 +529,10 @@
     )(snr_weight, diffusion_number, coupling, recombination.reshape(fields, 1))
 
     strips = lax.all_to_all(packed, "tile", 0, 0, tiled=True)
-    early = over_chips(strips[:, : rows[0]])
-    late = over_chips(hold(strips[:, rows[0] :], *[early[apart] for apart in sorted(early)[1:]], tables[4]))
-    early = over_cores(early)
+    early = over_chips(strips)
+    strips_late = lax.all_to_all(hold(packed_late, strips), "tile", 0, 0, tiled=True)
+    early = over_cores({apart: hold(early[apart], strips_late) if apart else early[apart] for apart in early})
+    late = over_chips(strips_late)
 
     work = [pltpu.VMEM(full, f32), pltpu.VMEM((levels * groups * tiles, lanes), f32)]
     known = pl.pallas_call(
@@ -542,18 +543,18 @@
             jax.ShapeDtypeStruct((count * groups * levels, lanes), f32),
             jax.ShapeDtypeStruct((2,) + cell, f32),
         ),
-        in_specs=[in_smem] + [in_vmem] * (parts + 5),
+        in_specs=[in_vmem] * (1 + parts + 5),
         out_specs=(in_vmem,) * 4,
         scratch_shapes=[pltpu.VMEM((parts * tiles * rows[0], lanes), f32)] + work,
         compiler_params=limit,
         cost_estimate=cost(5),
-    )(measure_step, *early, *tables)
+    )(measure_step.reshape(1, 1), *early, *tables)
 
     late = over_cores({apart: hold(late[apart], known[3]) if apart else late[apart] for apart in late})
     result = pl.pallas_call(
         functools.partial(late_kernel, dims, rows[1], steps - count, parts, out_rows),
         out_shape=jax.ShapeDtypeStruct((tiles, out_rows, lanes), jnp.int16),
-        in_specs=[in_smem] + [in_vmem] * (parts + 9),
+        in_specs=[in_vmem] * (1 + parts + 9),
         out_specs=in_vmem,
         scratch_shapes=[
             pltpu.VMEM((parts * tiles * rows[1], lanes), f32),
@@ -564,7 +565,7 @@
         + [pltpu.VMEM((tiles * out_rows, lanes), f32)],
         compiler_params=limit,
         cost_estimate=cost(5),
-    )(measure_step, *late, *tables, *known)
+    )(measure_step.reshape(1, 1), *late, *tables, *known)
     home = lax.all_to_all(result, "tile", 0, 0, tiled=True)
 
     state_adjoint, driver_grad = pl.pallas_call(

time: 61.8 us -> 65.4 us (1.058)
  blocking collectives: 34.1 us -> 30.6 us
  starting transfers between devices: 4.02 us -> 7.35 us
  waiting for transfers between devices: 5.09 us -> 7.74 us
  local copies, waits for them, and re-layouts: 0.15 us -> 1.06 us
    all_to_all x1, blocking collectives: 20.9 us -> 16.3 us  [per_device(): strips = lax.all_to_all(packed, 'tile', 0, 0, tiled=True)]
    all_to_all x0 -> x1, starting transfers between devices: none -> 3.59 us  [per_device(): lax.all_to_all(hold(packed_late, strips), 'tile', 0, 0, tiled=True)]
    pallas_call x1, Pallas kernels: 7.59 us -> 5.37 us  [per_device(): pl.pallas_call(functools.partial(late_kernel, dims, rows[1], steps - coun...]
    ppermute x6, waiting for transfers between devices: 5.09 us -> 7.07 us  [across(): lax.ppermute(value, 'obj', [(place, place ^ bit) for place in range(count)])]
    pallas_call x1, Pallas kernels: 4.95 us -> 6.56 us  [per_device(): pl.pallas_call(functools.partial(early_kernel, dims, rows[0], spots, coun...]
    all_to_all x1, blocking collectives: 13.2 us -> 14.3 us  [per_device(): home = lax.all_to_all(result, 'tile', 0, 0, tiled=True)]
    unnamed x8 -> x10, local copies, waits for them, and re-layouts: 0.03 us -> 0.96 us
    pallas_call x2 -> x3, Pallas kernels: 0.04 us -> 0.74 us  [hold(): pl.pallas_call(copy, out_shape=jax.ShapeDtypeStruct(value.shape, value.dt...]
  transfers between devices with their start and end apart: 6 -> 7, of which waited for: 4 -> 3; matrix products, arithmetic and copies ran while one was open for 0% -> 0% of each run, Pallas kernels for 9% -> 11%
where the time goes in v6:
time: 65.4 us; the launch traced here: 65 us
  blocking collectives  30.6 us (47%)
  Pallas kernels  16.8 us (26%)
  waiting for transfers between devices  7.74 us (12%)
  starting transfers between devices  7.35 us (11%)
  between operations  1.4 us (2%)
  local copies, waits for them, and re-layouts  1.06 us (2%)
    all_to_all x1, blocking collectives, per_device(): strips = lax.all_to_all(packed, 'tile', 0, 0, tiled=True)  16.3 us
    all_to_all x1, blocking collectives, per_device(): home = lax.all_to_all(result, 'tile', 0, 0, tiled=True)  14.3 us
    ppermute x6, waiting for transfers between devices, across(): lax.ppermute(value, 'obj', [(place, place ^ bit) for place in range(count)])  7.07 us
    pallas_call x1, Pallas kernels, per_device(): pl.pallas_call(functools.partial(early_kernel, dims, rows[0], spots, coun...  6.56 us
    pallas_call x1, Pallas kernels, per_device(): pl.pallas_call(functools.partial(late_kernel, dims, rows[1], steps - coun...  5.37 us
    ppermute x6, starting transfers between devices, across(): lax.ppermute(value, 'obj', [(place, place ^ bit) for place in range(count)])  3.76 us
    all_to_all x1, starting transfers between devices, per_device(): lax.all_to_all(hold(packed_late, strips), 'tile', 0, 0, tiled=True)  3.59 us
    pallas_call x1, Pallas kernels, per_device(): pl.pallas_call(functools.partial(pack_kernel, dims, rows, spots), out_sha...  2.46 us
  transfers between devices with their start and end apart: 7, of which 3 were waited for; matrix products, arithmetic and copies ran while one was open for 0% of the time, Pallas kernels for 11%

profile of v6, /device:TPU:0, one launch (start us, length us, event | category | flops | bytes accessed | tf_op | source)
XLA Modules:
  0.0 65.0 jit_solution(13378339588521050582)
XLA Ops:
  0.6 2.5 %shard_map.104 = (bf16[8,128,128]{2,1,0:T(8,128)(2,1)}, bf16[8,112,128]{2,1,0:T(8,128)(2,1)}) custom-call(bf16[6,12,12,128]{3,2,1,0:T(8,128)(2,1)} %bitcast.11, f32[2,48,128]{2,1,0:T(8,128)} %bitcast.12, f32[1,128]{1,0:T(1,128)} %refs_2_.1, s32[1,128]{1,0:T(1,128)} %bitcast.13), custom_call_target="tpu_custom_call" | custom-call | bytes 3000000 | tf_op jit(solution)/shard_map/pallas_call | solution.py:494
  3.1 0.0 copy-start.4
  3.1 0.0 copy-start.1
  3.1 0.0 copy-start.2
  3.1 0.0 copy-start.3
  3.1 16.3 %all_to_all.15.refs_0_ = bf16[8,128,128]{2,1,0:T(8,128)(2,1)S(1)} all-to-all(bf16[8,128,128]{2,1,0:T(8,128)(2,1)} %get-tuple-element.16), channel_id=1, replica_groups=mesh['obj'=4,'tile'=8] {'tile'}, dimensions={0} | all-to-all | bytes 524288 | tf_op jit(solution)/shard_map/all_to_all | solution.py:531
  19.5 0.0 copy-start
  19.5 0.9 %copy-done = bf16[8,112,128]{2,1,0:T(8,128)(2,1)S(1)} copy-done((bf16[8,112,128]{2,1,0:T(8,128)(2,1)S(1)}, bf16[8,112,128]{2,1,0:T(8,128)(2,1)}, u32[]{:S(2)}) %copy-start) | copy-done | bytes 229400
  20.4 0.7 %shard_map.105 = bf16[8,112,128]{2,1,0:T(8,128)(2,1)} custom-call(bf16[8,112,128]{2,1,0:T(8,128)(2,1)S(1)} %copy-done, bf16[8,128,128]{2,1,0:T(8,128)(2,1)S(1)} %all_to_all.15.refs_0_), custom_call_target="tpu_custom_call" | custom-call | tf_op jit(solution)/shard_map/pallas_call | solution.py:433
  21.1 3.6 %all-to-all-start.1 = ((bf16[8,112,128]{2,1,0:T(8,128)(2,1)}), bf16[8,112,128]{2,1,0:T(8,128)(2,1)S(1)}, u32[]{:S(2)}, u32[]{:S(2)}) async-start(bf16[8,112,128]{2,1,0:T(8,128)(2,1)} %shard_map.105), calls=%async_computation.1 | async-start | bytes 458752 | tf_op jit(solution)/shard_map/all_to_all | solution.py:533
  24.7 1.5 %collective-permute-start.3 = (bf16[8,128,128]{2,1,0:T(8,128)(2,1)S(1)}, bf16[8,128,128]{2,1,0:T(8,128)(2,1)S(1)}, u32[]{:S(2)}, u32[]{:S(2)}) collective-permute-start(bf16[8,128,128]{2,1,0:T(8,128)(2,1)S(1)} %all_to_all.15.refs_0_), channel_id=1, source_target_pairs={{0,16},{8,24},{16,0},{24,8},{1,17},{9,25},{17,1},{25,9},{2,18},{10... | collective-permute-start | bytes 786440 | tf_op jit(solution)/shard_map/ppermute | solution.py:425
  26.2 0.0 collective-permute-start.2
  26.2 5.9 %collective-permute-done.3.source = bf16[8,128,128]{2,1,0:T(8,128)(2,1)S(1)} collective-permute-done((bf16[8,128,128]{2,1,0:T(8,128)(2,1)S(1)}, bf16[8,128,128]{2,1,0:T(8,128)(2,1)S(1)}, u32[]{:S(2)}, u32[]{:S(2)}) %collective-permute-start.3) | collective-permute-done | bytes 262176 | tf_op jit(solution)/shard_map/ppermute | solution.py:425
  32.1 0.7 %all-to-all-done.1.refs_0_ = bf16[8,112,128]{2,1,0:T(8,128)(2,1)S(1)} async-done(((bf16[8,112,128]{2,1,0:T(8,128)(2,1)}), bf16[8,112,128]{2,1,0:T(8,128)(2,1)S(1)}, u32[]{:S(2)}, u32[]{:S(2)}) %all-to-all-start.1) | async-done | bytes 229408 | tf_op jit(solution)/shard_map/all_to_all | solution.py:533
  32.8 0.1 collective-permute-start.4
  32.9 1.6 %collective-permute-start.1 = (bf16[8,112,128]{2,1,0:T(8,128)(2,1)S(1)}, bf16[8,112,128]{2,1,0:T(8,128)(2,1)S(1)}, u32[]{:S(2)}, u32[]{:S(2)}) collective-permute-start(bf16[8,112,128]{2,1,0:T(8,128)(2,1)S(1)} %all-to-all-done.1.refs_0_), channel_id=1, source_target_pairs={{0,16},{8,24},{16,0},{24,8},{1,17},{9,25},{17,1},{25,9},{2,18},{10... | collective-permute-start | bytes 688136 | tf_op jit(solution)/shard_map/ppermute | solution.py:425
  34.5 0.0 copy-done.4
  34.5 0.1 copy.14.recombination
  35.2 0.0 copy-done.1
  35.2 0.0 copy-done.2
  35.2 0.0 copy-done.3
  35.2 0.5 shard_map.107
  35.8 0.2 collective-permute-start
  36.0 0.0 collective-permute-done.2.refs_1_
  36.0 0.0 collective-permute-done.4.refs_3_
  36.0 6.6 %shard_map.108 = (f32[144,16,128]{2,1,0:T(8,128)S(1)}, f32[48,4,8,128]{3,2,1,0:T(8,128)S(1)}, f32[432,128]{1,0:T(8,128)S(1)}, f32[2,8,128]{2,1,0:T(8,128)S(1)}) custom-call(s32[1,1]{1,0:T(1,128)} %bitcast.9.measure_step, bf16[8,128,128]{2,1,0:T(8,128)(2,1)S(1)} %all_to_all.15.refs_0_, bf16[8,128,128]{2,1,0:T(8,128)(2,1)S(1)} %collective-permute-done.2.refs_1_, ...), custom_call_target="tpu_custom_call" | custom-call | bytes 15000000 | tf_op jit(solution)/shard_map/pallas_call | solution.py:538
  42.6 0.0 collective-permute-done.1.source
  42.6 0.4 collective-permute-start.5
  43.0 0.0 collective-permute-done.refs_1_
  43.0 1.1 %collective-permute-done.5.refs_3_ = bf16[8,112,128]{2,1,0:T(8,128)(2,1)S(1)} collective-permute-done((bf16[8,112,128]{2,1,0:T(8,128)(2,1)S(1)}, bf16[8,112,128]{2,1,0:T(8,128)(2,1)S(1)}, u32[]{:S(2)}, u32[]{:S(2)}) %collective-permute-start.5) | collective-permute-done | bytes 229408 | tf_op jit(solution)/shard_map/ppermute | solution.py:425
  44.2 5.4 %shard_map.110 = s16[8,128,128]{2,1,0:T(8,128)(2,1)S(1)} custom-call(s32[1,1]{1,0:T(1,128)} %bitcast.10.measure_step, bf16[8,112,128]{2,1,0:T(8,128)(2,1)S(1)} %all-to-all-done.1.refs_0_, bf16[8,112,128]{2,1,0:T(8,128)(2,1)S(1)} %collective-permute-done.refs_1_, bf16[8,112,128]{2,1,0:T(8,128)(2,1)S(1)} %shard_map.109.refs_2_, ...), custom_call_target="tpu_custom_call" | custom-call | bytes 15000000 | tf_op jit(solution)/shard_map/pallas_call | solution.py:554
  49.6 14.3 %all_to_all.16.arrived = s16[8,128,128]{2,1,0:T(8,128)(2,1)S(1)} all-to-all(s16[8,128,128]{2,1,0:T(8,128)(2,1)S(1)} %shard_map.110), channel_id=1, replica_groups=mesh['obj'=4,'tile'=8] {'tile'}, dimensions={0} | all-to-all | bytes 524288 | tf_op jit(solution)/shard_map/all_to_all | solution.py:569
  63.8 1.1 %shard_map.111 = (f32[576,128]{1,0:T(8,128)}, f32[72,48]{1,0:T(8,128)}) custom-call(s16[8,128,128]{2,1,0:T(8,128)(2,1)S(1)} %all_to_all.16.arrived), custom_call_target="tpu_custom_call" | custom-call | tf_op jit(solution)/shard_map/pallas_call | solution.py:571
  (2 shorter events, 0.0 us)
Async XLA Ops:
  3.1 31.4 %copy-start.4 = (f32[12]{0:T(128)S(1)}, f32[12]{0:T(128)}, u32[]{:S(2)}) copy-start(f32[12]{0:T(128)} %param.17) | copy-start | bytes 148
  3.1 32.1 %copy-start.1 = (f32[12,48]{1,0:T(8,128)S(1)}, f32[12,48]{1,0:T(8,128)}, u32[]{:S(2)}) copy-start(f32[12,48]{1,0:T(8,128)} %snr_weight.1) | copy-start | bytes 6916
  3.1 32.1 %copy-start.2 = (f32[12,47]{1,0:T(8,128)S(1)}, f32[12,47]{1,0:T(8,128)}, u32[]{:S(2)}) copy-start(f32[12,47]{1,0:T(8,128)} %diffusion.1) | copy-start | bytes 6772
  3.1 32.1 %copy-start.3 = (f32[12,12]{1,0:T(8,128)S(1)}, f32[12,12]{1,0:T(8,128)}, u32[]{:S(2)}) copy-start(f32[12,12]{1,0:T(8,128)} %coupling.1) | copy-start | bytes 1732
  19.5 0.9 %copy-start = (bf16[8,112,128]{2,1,0:T(8,128)(2,1)S(1)}, bf16[8,112,128]{2,1,0:T(8,128)(2,1)}, u32[]{:S(2)}) copy-start(bf16[8,112,128]{2,1,0:T(8,128)(2,1)} %get-tuple-element.15.source) | copy-start | bytes 688132
  21.1 11.7 %all-to-all-start.1 = ((bf16[8,112,128]{2,1,0:T(8,128)(2,1)}), bf16[8,112,128]{2,1,0:T(8,128)(2,1)S(1)}, u32[]{:S(2)}, u32[]{:S(2)}) async-start(bf16[8,112,128]{2,1,0:T(8,128)(2,1)} %shard_map.105), calls=%async_computation.1 | async-start | bytes 458752 | tf_op jit(solution)/shard_map/all_to_all | solution.py:533
  24.7 7.4 %collective-permute-start.3 = (bf16[8,128,128]{2,1,0:T(8,128)(2,1)S(1)}, bf16[8,128,128]{2,1,0:T(8,128)(2,1)S(1)}, u32[]{:S(2)}, u32[]{:S(2)}) collective-permute-start(bf16[8,128,128]{2,1,0:T(8,128)(2,1)S(1)} %all_to_all.15.refs_0_), channel_id=1, source_target_pairs={{0,16},{8,24},{16,0},{24,8},{1,17},{9,25},{17,1},{25,9},{2,18},{10... | collective-permute-start | bytes 786440 | tf_op jit(solution)/shard_map/ppermute | solution.py:425
  26.2 9.8 %collective-permute-start.2 = (bf16[8,128,128]{2,1,0:T(8,128)(2,1)S(1)}, bf16[8,128,128]{2,1,0:T(8,128)(2,1)S(1)}, u32[]{:S(2)}, u32[]{:S(2)}) collective-permute-start(bf16[8,128,128]{2,1,0:T(8,128)(2,1)S(1)} %all_to_all.15.refs_0_), channel_id=1, source_target_pairs={{0,8},{8,0},{16,24},{24,16},{1,9},{9,1},{17,25},{25,17},{2,10},{10... | collective-permute-start | bytes 786440 | tf_op jit(solution)/shard_map/ppermute | solution.py:425
  32.8 3.2 %collective-permute-start.4 = (bf16[8,128,128]{2,1,0:T(8,128)(2,1)S(1)}, bf16[8,128,128]{2,1,0:T(8,128)(2,1)S(1)}, u32[]{:S(2)}, u32[]{:S(2)}) collective-permute-start(bf16[8,128,128]{2,1,0:T(8,128)(2,1)S(1)} %shard_map.106.refs_2_), channel_id=1, source_target_pairs={{0,8},{8,0},{16,24},{24,16},{1,9},{9,1},{17,25},{25,17},{2,10},{10... | collective-permute-start | bytes 786440 | tf_op jit(solution)/shard_map/ppermute | solution.py:425
  32.9 9.7 %collective-permute-start.1 = (bf16[8,112,128]{2,1,0:T(8,128)(2,1)S(1)}, bf16[8,112,128]{2,1,0:T(8,128)(2,1)S(1)}, u32[]{:S(2)}, u32[]{:S(2)}) collective-permute-start(bf16[8,112,128]{2,1,0:T(8,128)(2,1)S(1)} %all-to-all-done.1.refs_0_), channel_id=1, source_target_pairs={{0,16},{8,24},{16,0},{24,8},{1,17},{9,25},{17,1},{25,9},{2,18},{10... | collective-permute-start | bytes 688136 | tf_op jit(solution)/shard_map/ppermute | solution.py:425
  35.8 7.3 %collective-permute-start = (bf16[8,112,128]{2,1,0:T(8,128)(2,1)S(1)}, bf16[8,112,128]{2,1,0:T(8,128)(2,1)S(1)}, u32[]{:S(2)}, u32[]{:S(2)}) collective-permute-start(bf16[8,112,128]{2,1,0:T(8,128)(2,1)S(1)} %all-to-all-done.1.refs_0_), channel_id=1, source_target_pairs={{0,8},{8,0},{16,24},{24,16},{1,9},{9,1},{17,25},{25,17},{2,10},{10... | collective-permute-start | bytes 688136 | tf_op jit(solution)/shard_map/ppermute | solution.py:425
  42.6 1.6 %collective-permute-start.5 = (bf16[8,112,128]{2,1,0:T(8,128)(2,1)S(1)}, bf16[8,112,128]{2,1,0:T(8,128)(2,1)S(1)}, u32[]{:S(2)}, u32[]{:S(2)}) collective-permute-start(bf16[8,112,128]{2,1,0:T(8,128)(2,1)S(1)} %shard_map.109.refs_2_), channel_id=1, source_target_pairs={{0,8},{8,0},{16,24},{24,16},{1,9},{9,1},{17,25},{25,17},{2,10},{10... | collective-permute-start | bytes 688136 | tf_op jit(solution)/shard_map/ppermute | solution.py:425
